TPU v7x, 32 devices: a whole 2x2x4 slice. The times are simulated.
32 devices in a mesh: dp: 16 (over z, y, x), tensor: 2 (over core).
Axes of the slice: x: 2, y: 2, z: 4, core: 2. Of those that a mesh axis runs over, the one named last changes fastest.
Arguments:
- inputs: bfloat16 [32768, 768], P(('dp', 'tensor')), may hold values from -6 to 6
- out_grad: bfloat16 [32768, 768], P(('dp', 'tensor')), may hold values from -6 to 6
- lengths: int32 [16], P('dp'), may hold values from 1025 to 2048
- w_qkv: bfloat16 [3, 768, 768], P(None, 'dp', 'tensor'), may hold values from -0.21875 to 0.21875
- w_out: bfloat16 [768, 768], P('tensor', 'dp'), may hold values from -1.75 to 1.75
- w_up: bfloat16 [768, 3072], P('dp', 'tensor'), may hold values from -0.21875 to 0.21875
- w_down: bfloat16 [3072, 768], P('tensor', 'dp'), may hold values from -0.109375 to 0.109375
- gains: bfloat16 [2, 768], replicated, may hold values from 0.099609375 to 1.8984375
- shifts: bfloat16 [4, 768], replicated, may hold values from -3 to 3
- ff_bias: bfloat16 [3072], P('tensor'), may hold values from -3 to 3
Outputs:
- out: bfloat16 [32768, 768], P(('dp', 'tensor'))
- grad_inputs: float32 [32768, 768], P(('dp', 'tensor'))
- grad_qkv: float32 [3, 768, 768], P(None, 'dp', 'tensor')
- grad_out_proj: float32 [768, 768], P('tensor', 'dp')
- grad_up: float32 [768, 3072], P('dp', 'tensor')
- grad_down: float32 [3072, 768], P('tensor', 'dp')
- grad_gains: float32 [2, 768], replicated
- grad_shifts: float32 [4, 768], replicated
- grad_ff_bias: float32 [3072], P('tensor')
All inputs are finite; a program needn't handle non-finite values.
Results may differ from a plain program's by a relative error of at most 0.015.
The roundings to bfloat16 on the way count: a program that leaves them out, or rounds other values in their place, can miss the bound.
Values may be sent and summed in bfloat16 or wider, within the bound.
A program may use at most 192 MiB of HBM per device.

v0:
```python
import jax
import jax.numpy as jnp
from jax import lax
from jax.sharding import PartitionSpec as P

HD = 64
LEN = 2048


norm_eps = 1e-06
masked_score = -1e30


def layer_norm(hidden, gain, shift):
    center = hidden - jnp.mean(hidden, axis=-1, keepdims=True)
    spread = jnp.mean(center * center, axis=-1, keepdims=True)
    return center * lax.rsqrt(spread + norm_eps) * gain + shift


def exact_gelu(ff_pre):
    return jax.nn.gelu(ff_pre, approximate=False)


def softmax_rows(query_block, key_rows, key_mask):
    scores = jnp.einsum("qd,kd->qk", query_block, key_rows, preferred_element_type=jnp.float32)
    scores = jnp.where(key_mask[None, :], scores, masked_score)
    row_max = jnp.max(scores, axis=-1, keepdims=True)
    shifted = jnp.exp(scores - row_max)
    return shifted / jnp.sum(shifted, axis=-1, keepdims=True)


def heads_first(matrix, seq_count, head_count):
    return (
        matrix.reshape(seq_count, LEN, head_count, HD)
        .transpose(0, 2, 1, 3)
        .reshape(seq_count * head_count, LEN, HD)
    )


def heads_last(stacked, seq_count, head_count):
    return (
        stacked.reshape(seq_count, head_count, LEN, HD)
        .transpose(0, 2, 1, 3)
        .reshape(seq_count * LEN, head_count * HD)
    )


def attend_forward(member):
    query_rows, key_rows, value_rows, seq_len = member
    key_mask = jnp.arange(LEN, dtype=jnp.int32) < seq_len
    block_rows = min(512, LEN)

    def one_block(query_block):
        attn_probs = softmax_rows(query_block, key_rows, key_mask)
        return jnp.dot(
            attn_probs.astype(jnp.bfloat16), value_rows, preferred_element_type=jnp.float32
        )

    context = lax.map(one_block, query_rows.reshape(LEN // block_rows, block_rows, HD))
    return context.reshape(LEN, HD)


def attend_backward(member):
    query_rows, key_rows, value_rows, ctx_rows, seq_len = member
    key_mask = jnp.arange(LEN, dtype=jnp.int32) < seq_len
    block_rows = min(512, LEN)

    def one_step(totals, blocks):
        key_total, value_total = totals
        query_block, ctx_block = blocks
        attn_probs = softmax_rows(query_block, key_rows, key_mask)
        prob_grad = jnp.einsum(
            "qd,kd->qk", ctx_block, value_rows, preferred_element_type=jnp.float32
        )
        delta = jnp.sum(attn_probs * prob_grad, axis=-1, keepdims=True)
        score_grad = (attn_probs * (prob_grad - delta)).astype(jnp.bfloat16)
        query_part = jnp.einsum(
            "qk,kd->qd", score_grad, key_rows, preferred_element_type=jnp.float32
        )
        key_total = key_total + jnp.einsum(
            "qk,qd->kd", score_grad, query_block, preferred_element_type=jnp.float32
        )
        value_total = value_total + jnp.einsum(
            "qk,qd->kd",
            attn_probs.astype(jnp.bfloat16),
            ctx_block,
            preferred_element_type=jnp.float32,
        )
        return ((key_total, value_total), query_part)

    zeros_init = jnp.zeros((LEN, HD), jnp.float32)
    shaped = (LEN // block_rows, block_rows, HD)
    (key_grad, value_grad), query_grad = lax.scan(
        one_step, (zeros_init, zeros_init), (query_rows.reshape(shaped), ctx_rows.reshape(shaped))
    )
    return (query_grad.reshape(LEN, HD), key_grad, value_grad)


def body(inputs, out_grad, lengths, w_qkv, w_out, w_up, w_down, gains, shifts, ff_bias):
    score_scale = HD ** (-0.5)
    seq_count = lengths.shape[0]
    head_count = w_qkv.shape[2] // HD
    gains_f = gains.astype(jnp.float32)
    shifts_f = shifts.astype(jnp.float32)
    inputs_f = inputs.astype(jnp.float32)
    gathered = lax.all_gather(inputs, "tensor", axis=0, tiled=True)
    qkv_full, out_full = (
        lax.all_gather(w_qkv, "dp", axis=1, tiled=True),
        lax.all_gather(w_out, "dp", axis=1, tiled=True),
    )
    projected = jnp.einsum("rd,cde->cre", gathered, qkv_full, preferred_element_type=jnp.float32)
    queries = (projected[0] * score_scale).astype(jnp.bfloat16)
    keys_all = projected[1].astype(jnp.bfloat16)
    values_all = projected[2].astype(jnp.bfloat16)
    head_lens = jnp.repeat(lengths, head_count)
    query_heads = heads_first(queries, seq_count, head_count)
    key_heads = heads_first(keys_all, seq_count, head_count)
    value_heads = heads_first(values_all, seq_count, head_count)
    context_f = lax.map(attend_forward, (query_heads, key_heads, value_heads, head_lens))
    context = heads_last(context_f, seq_count, head_count).astype(jnp.bfloat16)
    attn_branch = (
        lax.psum_scatter(
            jnp.dot(context, out_full, preferred_element_type=jnp.float32),
            "tensor",
            scatter_dimension=0,
            tiled=True,
        )
        + shifts_f[0]
    )
    resid_one = inputs_f + attn_branch
    normed_f, norm_one_back = jax.vjp(layer_norm, resid_one, gains_f[0], shifts_f[1])
    normed_one = normed_f.astype(jnp.bfloat16)
    normed_all = lax.all_gather(normed_one, "tensor", axis=0, tiled=True)
    up_full, down_full = (
        lax.all_gather(w_up, "dp", axis=0, tiled=True),
        lax.all_gather(w_down, "dp", axis=1, tiled=True),
    )
    ff_pre = jnp.dot(normed_all, up_full, preferred_element_type=jnp.float32) + ff_bias.astype(
        jnp.float32
    )
    ff_act_f, gelu_back = jax.vjp(exact_gelu, ff_pre)
    ff_act = ff_act_f.astype(jnp.bfloat16)
    mlp_branch = (
        lax.psum_scatter(
            jnp.dot(ff_act, down_full, preferred_element_type=jnp.float32),
            "tensor",
            scatter_dimension=0,
            tiled=True,
        )
        + shifts_f[2]
    )
    resid_two = normed_one.astype(jnp.float32) + mlp_branch
    result, norm_two_back = jax.vjp(layer_norm, resid_two, gains_f[1], shifts_f[3])
    resid_two_grad, gain_two_grad, shift_three_grad = norm_two_back(out_grad.astype(jnp.float32))
    mlp_grad = resid_two_grad.astype(jnp.bfloat16)
    shift_two_grad = jnp.sum(mlp_grad.astype(jnp.float32), axis=0)
    mlp_grad_all = lax.all_gather(mlp_grad, "tensor", axis=0, tiled=True)
    act_grad = jnp.einsum("rd,fd->rf", mlp_grad_all, down_full, preferred_element_type=jnp.float32)
    down_grad = jnp.einsum("rf,rd->fd", ff_act, mlp_grad_all, preferred_element_type=jnp.float32)
    pre_grad = gelu_back(act_grad)[0].astype(jnp.bfloat16)
    bias_grad = jnp.sum(pre_grad.astype(jnp.float32), axis=0)
    up_grad = jnp.einsum("rd,rf->df", normed_all, pre_grad, preferred_element_type=jnp.float32)
    slab_rows = pre_grad
    normed_grad = resid_two_grad + lax.psum_scatter(
        jnp.einsum("rf,df->rd", slab_rows, up_full, preferred_element_type=jnp.float32),
        "tensor",
        scatter_dimension=0,
        tiled=True,
    )
    resid_one_grad, gain_one_grad, shift_one_grad = norm_one_back(normed_grad)
    attn_grad = resid_one_grad.astype(jnp.bfloat16)
    shift_zero_grad = jnp.sum(attn_grad.astype(jnp.float32), axis=0)
    attn_grad_all = lax.all_gather(attn_grad, "tensor", axis=0, tiled=True)
    context_grad = jnp.einsum(
        "rd,ed->re", attn_grad_all, out_full, preferred_element_type=jnp.float32
    ).astype(jnp.bfloat16)
    out_proj_grad = jnp.einsum(
        "re,rd->ed", context, attn_grad_all, preferred_element_type=jnp.float32
    )
    ctx_heads = heads_first(context_grad, seq_count, head_count)
    query_grad, key_grad, value_grad = lax.map(
        attend_backward, (query_heads, key_heads, value_heads, ctx_heads, head_lens)
    )
    stacked_grad = jnp.stack(
        [
            heads_last(query_grad, seq_count, head_count),
            heads_last(key_grad, seq_count, head_count),
            heads_last(value_grad, seq_count, head_count),
        ]
    ).astype(jnp.bfloat16)
    qkv_scale = jnp.array([score_scale, 1.0, 1.0], jnp.float32)
    qkv_grad = (
        jnp.einsum("rd,cre->cde", gathered, stacked_grad, preferred_element_type=jnp.float32)
        * qkv_scale[:, None, None]
    )
    qkv_owned, out_owned, up_owned, down_owned = (
        lax.psum_scatter(qkv_grad, "dp", scatter_dimension=1, tiled=True),
        lax.psum_scatter(out_proj_grad, "dp", scatter_dimension=1, tiled=True),
        lax.psum_scatter(up_grad, "dp", scatter_dimension=0, tiled=True),
        lax.psum_scatter(down_grad, "dp", scatter_dimension=1, tiled=True),
    )
    slab_rows = stacked_grad
    parts = jnp.einsum("cre,cde->crd", slab_rows, qkv_full, preferred_element_type=jnp.float32)
    input_grad = resid_one_grad + lax.psum_scatter(
        (parts[0] * score_scale + parts[1] + parts[2]).astype(jnp.bfloat16),
        "tensor",
        scatter_dimension=0,
        tiled=True,
    ).astype(jnp.float32)
    gain_grads = jnp.stack([gain_one_grad, gain_two_grad])
    shift_grads = jnp.stack([shift_zero_grad, shift_one_grad, shift_two_grad, shift_three_grad])
    tensor_count = lax.axis_size("tensor")
    own_slot = (jnp.arange(tensor_count, dtype=jnp.int32) == lax.axis_index("tensor")).astype(
        jnp.float32
    )
    spread_bias = own_slot[:, None] * bias_grad[None, :]
    gain_sum, shift_sum, bias_sum = lax.psum(
        (gain_grads, shift_grads, spread_bias), ("dp", "tensor")
    )
    bias_owned = jnp.sum(own_slot[:, None] * bias_sum, axis=0)
    return (
        result.astype(jnp.bfloat16),
        input_grad,
        qkv_owned,
        out_owned,
        up_owned,
        down_owned,
        gain_sum,
        shift_sum,
        bias_owned,
    )


def solution(mesh):
    return jax.shard_map(
        body,
        mesh=mesh,
        in_specs=(
            P(("dp", "tensor"), None),
            P(("dp", "tensor"), None),
            P("dp"),
            P(None, "dp", "tensor"),
            P("tensor", "dp"),
            P("dp", "tensor"),
            P("tensor", "dp"),
            P(),
            P(),
            P("tensor"),
        ),
        out_specs=(
            P(("dp", "tensor"), None),
            P(("dp", "tensor"), None),
            P(None, "dp", "tensor"),
            P("tensor", "dp"),
            P("dp", "tensor"),
            P("tensor", "dp"),
            P(),
            P(),
            P("tensor"),
        ),
        check_vma=False,
    )
```

profile of v0, /device:TPU:12, one launch (start us, length us, event | category | flops | bytes accessed | tf_op | source)
XLA Modules:
  0.0 1466.3 jit_solution(2063813809935758152)
XLA Ops:
  9.4 37.6 %all_gather.26 = bf16[384,768]{0,1:T(8,128)(2,1)} all-gather(bf16[384,48]{0,1:T(8,128)(2,1)} %param.23), channel_id=1, replica_groups=mesh['dp'=16,'tensor'=2] {'dp'}, dimensions={1}, use_global_device_ids=true | all-gather | bytes 626688 | tf_op jit(solution)/shard_map/all_gather | solution.py:109
  46.9 38.3 %all-gather.8.cloned.1.call-done = bf16[3,768,384]{2,1,0:T(8,128)(2,1)} async-done(((bf16[3,48,384]{2,1,0:T(8,128)(2,1)}), bf16[3,768,384]{2,1,0:T(8,128)(2,1)}) %all-gather.8.cloned.1.call-update) | async-done | bytes 1769488 | tf_op jit(solution)/shard_map/all_gather | solution.py:108
  85.2 9.9 fusion.61
  106.0 103.9 %while.51 = (s32[]{:T(128)}, bf16[6,2048,64]{1,2,0:T(8,128)(2,1)S(1)}, bf16[6,2048,64]{2,1,0:T(8,128)(2,1)}, bf16[6,2048,64]{2,1,0:T(8,128)(2,1)}, s32[6]{0:T(12...) while((s32[]{:T(128)}, bf16[6,2048,64]{1,2,0:T(8,128)(2,1)S(1)}, ...), condition=%wide.region_5.6_spmd, body=%wide.region_0.5_spmd.sunk | while | flops 277873664 | bytes 17058060 | solution.py:119
  108.9 13.8 while.54
  126.3 13.8 while.54
  143.6 13.8 while.54
  160.9 13.8 while.54
  178.2 13.8 while.54
  195.6 13.8 while.54
  209.9 6.0 fusion.62
  217.2 13.0 reduce-scatter.8.cloned.1.call-done
  236.5 60.4 %all-gather.14.cloned.1.call-done = bf16[768,1536]{1,0:T(8,128)(2,1)} async-done(((bf16[48,1536]{1,0:T(8,128)(2,1)}), bf16[768,1536]{1,0:T(8,128)(2,1)}) %all-gather.14.cloned.1.call-update) | async-done | bytes 2359312 | tf_op jit(solution)/shard_map/all_gather | solution.py:135
  296.9 12.9 all-gather.12.cloned.1.call-done
  309.8 34.9 %multiply_convert_fusion.1 = (bf16[2048,1536]{1,0:T(8,128)(2,1)}, f32[2048,1536]{1,0:T(8,128)}, f32[2048,1536]{1,0:T(8,128)}) fusion(f32[1536]{0:T(1024)S(1)} %convert_element_type.134, bf16[2048,768]{1,0:T(8,128)(2,1)} %all-gather.12.cloned.1.call-done, bf16[768,1536]{1,0:T(8,128)(2,1)} %all-gather.14.cloned.1.call-done), kind=kOutput, calls=%fused_computation.56 | convolution fusion | flops 5039456256 | bytes 36968448 | tf_op jit(solution)/shard_map/dot_general | solution.py:138
  344.6 31.8 %all-gather.16.cloned.1.call-done = bf16[1536,768]{0,1:T(8,128)(2,1)} async-done(((bf16[1536,48]{0,1:T(8,128)(2,1)}), bf16[1536,768]{0,1:T(8,128)(2,1)}) %all-gather.16.cloned.1.call-update) | async-done | bytes 2359312 | tf_op jit(solution)/shard_map/all_gather | solution.py:136
  376.5 9.6 fusion.63
  386.3 13.1 reduce-scatter.10.cloned.1.call-done
  411.9 13.4 all-gather.18.cloned.1.call-done
  425.3 17.6 %convert_reduce_fusion = (f32[1536]{0:T(1024)}, bf16[2048,1536]{1,0:T(8,128)(2,1)S(1)}) fusion(f32[2048,1536]{1,0:T(8,128)} %get-tuple-element.382, bf16[2048,768]{1,0:T(8,128)(2,1)} %all-gather.18.cloned.1.call-done, bf16[1536,768]{0,1:T(8,128)(2,1)} %all-gather.16.cloned.1.call-done, f32[2048,1536]{1,0:T(8,128)} %get-tuple-element.400, ...), kind=kOutput, calls=%fused_computation.54 | convolution fusion | flops 4885314048 | bytes 36974592 | tf_op jit(solution)/shard_map/rd,fd->rf/dot_general | solution.py:158
  445.5 6.9 fusion.64
  452.5 15.8 %reduce-scatter.12.cloned.1.call-done = f32[1024,768]{1,0:T(8,128)} async-done(((f32[2048,768]{1,0:T(8,128)}), f32[1024,768]{1,0:T(8,128)}) %reduce-scatter.12.cloned.1.call-update) | async-done | bytes 3145744 | tf_op jit(solution)/shard_map/reduce_scatter | solution.py:164
  468.3 4.3 multiply_reduce_fusion.1
  477.9 13.4 all-gather.20.cloned.1.call-done
  501.9 328.2 %while.53 = (s32[]{:T(128)}, bf16[6,2048,64]{1,2,0:T(8,128)(2,1)}, bf16[6,2048,64]{1,2,0:T(8,128)(2,1)}, bf16[6,2048,64]{1,2,0:T(8,128)(2,1)}, bf16[6,2048,64]{2...) while((s32[]{:T(128)}, bf16[6,2048,64]{1,2,0:T(8,128)(2,1)}, ...), condition=%wide.region_23.24_spmd, body=%wide.region_17.23_spmd.sunk | while | flops 692584960 | bytes 79334840 | solution.py:181
  506.8 47.7 %while.55 = (s32[]{:T(128)}, f32[2048,64]{0,1:T(8,128)S(1)}, f32[2048,64]{0,1:T(8,128)S(1)}, bf16[4,512,64]{1,2,0:T(8,128)(2,1)S(1)}, bf16[4,512,64]{2,1,0:T(8,1...) while((s32[]{:T(128)}, f32[2048,64]{0,1:T(8,128)S(1)}, ...), condition=%wide.region_22.22_spmd.clone, body=%wide.region_18.21_spmd.clone.sunk | while | flops 692584960 | bytes 73566400 | solution.py:93
  535.0 3.5 convolution_add_fusion.5
  546.9 3.5 convolution_add_fusion.5
  561.5 47.7 %while.55 = (s32[]{:T(128)}, f32[2048,64]{0,1:T(8,128)S(1)}, f32[2048,64]{0,1:T(8,128)S(1)}, bf16[4,512,64]{1,2,0:T(8,128)(2,1)S(1)}, bf16[4,512,64]{2,1,0:T(8,1...) while((s32[]{:T(128)}, f32[2048,64]{0,1:T(8,128)S(1)}, ...), condition=%wide.region_22.22_spmd.clone, body=%wide.region_18.21_spmd.clone.sunk | while | flops 692584960 | bytes 73566400 | solution.py:93
  601.6 3.5 convolution_add_fusion.5
  616.3 47.7 %while.55 = (s32[]{:T(128)}, f32[2048,64]{0,1:T(8,128)S(1)}, f32[2048,64]{0,1:T(8,128)S(1)}, bf16[4,512,64]{1,2,0:T(8,128)(2,1)S(1)}, bf16[4,512,64]{2,1,0:T(8,1...) while((s32[]{:T(128)}, f32[2048,64]{0,1:T(8,128)S(1)}, ...), condition=%wide.region_22.22_spmd.clone, body=%wide.region_18.21_spmd.clone.sunk | while | flops 692584960 | bytes 73566400 | solution.py:93
  620.6 3.5 convolution_add_fusion.5
  632.5 3.5 convolution_add_fusion.5
  671.0 47.7 %while.55 = (s32[]{:T(128)}, f32[2048,64]{0,1:T(8,128)S(1)}, f32[2048,64]{0,1:T(8,128)S(1)}, bf16[4,512,64]{1,2,0:T(8,128)(2,1)S(1)}, bf16[4,512,64]{2,1,0:T(8,1...) while((s32[]{:T(128)}, f32[2048,64]{0,1:T(8,128)S(1)}, ...), condition=%wide.region_22.22_spmd.clone, body=%wide.region_18.21_spmd.clone.sunk | while | flops 692584960 | bytes 73566400 | solution.py:93
  725.6 47.7 %while.55 = (s32[]{:T(128)}, f32[2048,64]{0,1:T(8,128)S(1)}, f32[2048,64]{0,1:T(8,128)S(1)}, bf16[4,512,64]{1,2,0:T(8,128)(2,1)S(1)}, bf16[4,512,64]{2,1,0:T(8,1...) while((s32[]{:T(128)}, f32[2048,64]{0,1:T(8,128)S(1)}, ...), condition=%wide.region_22.22_spmd.clone, body=%wide.region_18.21_spmd.clone.sunk | while | flops 692584960 | bytes 73566400 | solution.py:93
  780.4 47.7 %while.55 = (s32[]{:T(128)}, f32[2048,64]{0,1:T(8,128)S(1)}, f32[2048,64]{0,1:T(8,128)S(1)}, bf16[4,512,64]{1,2,0:T(8,128)(2,1)S(1)}, bf16[4,512,64]{2,1,0:T(8,1...) while((s32[]{:T(128)}, f32[2048,64]{0,1:T(8,128)S(1)}, ...), condition=%wide.region_22.22_spmd.clone, body=%wide.region_18.21_spmd.clone.sunk | while | flops 692584960 | bytes 73566400 | solution.py:93
  836.5 8.2 multiply_bitcast_fusion
  844.7 6.3 copy.78
  851.2 7.1 fusion.50
  862.6 9.5 fusion.67
  874.1 9.6 fusion.66
  883.9 5.5 fusion.65
  890.8 42.6 %all-reduce.1 = (f32[2,768]{1,0:T(2,128)}, f32[4,768]{1,0:T(4,128)}, f32[2,1536]{1,0:T(2,128)S(1)}) all-reduce(f32[2,768]{1,0:T(2,128)S(1)} %pad_maximum_fusion.4, f32[4,768]{1,0:T(4,128)S(1)} %pad_maximum_fusion.3, f32[2,1536]{1,0:T(2,128)S(1)} %broadcast_multiply_fusion), channel_id=1, replica_groups=mesh['dp'=16,'tensor'=2] {'dp','tensor'}, use_global_device_ids=true, to_apply=%region_31.32 | all-reduce | flops 7680 | bytes 61440 | tf_op jit(solution)/shard_map/psum | solution.py:217
  934.1 96.6 %all-reduce.4.cloned.1.call-done = f32[3,768,384]{2,0,1:T(4,128)} async-done(((f32[3,768,384]{2,0,1:T(4,128)}), f32[3,768,384]{2,0,1:T(4,128)}) %all-reduce.4.cloned.1.call-update) | async-done | bytes 3538960
  1032.4 12.6 reduce-scatter.14.cloned.1.call-done
  1048.4 140.9 %reduce-scatter.20.cloned.1.call-done = f32[1536,48]{0,1:T(8,128)} async-done(((f32[1536,768]{0,1:T(8,128)}), f32[1536,48]{0,1:T(8,128)}) %reduce-scatter.20.cloned.1.call-update) | async-done | bytes 294928 | tf_op jit(solution)/shard_map/reduce_scatter | solution.py:200
  1189.4 141.7 %reduce-scatter.18.cloned.1.call-done = f32[48,1536]{1,0:T(8,128)} async-done(((f32[768,1536]{1,0:T(8,128)}), f32[48,1536]{1,0:T(8,128)}) %reduce-scatter.18.cloned.1.call-update) | async-done | bytes 294928 | tf_op jit(solution)/shard_map/reduce_scatter | solution.py:199
  1331.0 128.6 %reduce-scatter.16.cloned.1.call-done = f32[384,48]{0,1:T(8,128)} async-done(((f32[384,768]{0,1:T(8,128)}), f32[384,48]{0,1:T(8,128)}) %reduce-scatter.16.cloned.1.call-update) | async-done | bytes 73744 | tf_op jit(solution)/shard_map/reduce_scatter | solution.py:198
  (634 shorter events, 482.5 us)
Async XLA Ops:
  7.2 39.8 %all-gather.10.cloned.1.call-start = ((), (), s32[]{:S(2)}) async-start(), calls=%async_computation.8 | async-start | bytes 4718592 | tf_op jit(solution)/shard_map/all_gather | solution.py:106
  7.9 77.3 %all-gather.8.cloned.1.call-start = ((), (), s32[]{:S(2)}) async-start(), calls=%async_computation.7 | async-start | bytes 1880064 | tf_op jit(solution)/shard_map/all_gather | solution.py:108
  8.7 221.6 %reduce-scatter.8.cloned.1.call-start = ((), (), s32[]{:S(2)}) async-start(), calls=%async_computation.9 | async-start | bytes 9437184 | tf_op jit(solution)/shard_map/reduce_scatter | solution.py:122
  209.9 6.0 copy-start.5
  209.9 6.0 copy-start.26
  216.0 80.9 %all-gather.14.cloned.1.call-start = ((), (), s32[]{:S(2)}) async-start(), calls=%async_computation.11 | async-start | bytes 2506752 | tf_op jit(solution)/shard_map/all_gather | solution.py:135
  216.6 93.2 %all-gather.12.cloned.1.call-start = ((), (), s32[]{:S(2)}) async-start(), calls=%async_computation.10 | async-start | bytes 4718592 | tf_op jit(solution)/shard_map/all_gather | solution.py:133
  235.9 140.6 %all-gather.16.cloned.1.call-start = ((), (), s32[]{:S(2)}) async-start(), calls=%async_computation.12 | async-start | bytes 2506752 | tf_op jit(solution)/shard_map/all_gather | solution.py:136
  236.5 163.0 %reduce-scatter.10.cloned.1.call-start = ((), (), s32[]{:S(2)}) async-start(), calls=%async_computation.13 | async-start | bytes 9437184 | tf_op jit(solution)/shard_map/reduce_scatter | solution.py:144
  386.1 39.2 %all-gather.18.cloned.1.call-start = ((), (), s32[]{:S(2)}) async-start(), calls=%async_computation.14 | async-start | bytes 4718592 | tf_op jit(solution)/shard_map/all_gather | solution.py:157
  411.9 56.4 %reduce-scatter.12.cloned.1.call-start = ((), (), s32[]{:S(2)}) async-start(), calls=%async_computation.15 | async-start | bytes 9437184 | tf_op jit(solution)/shard_map/reduce_scatter | solution.py:164
  425.3 20.2 %copy-start.24 = (bf16[768,1536]{1,0:T(8,128)(2,1)S(1)}, bf16[768,1536]{1,0:T(8,128)(2,1)}, u32[]{:S(2)}) copy-start(bf16[768,1536]{1,0:T(8,128)(2,1)} %all-gather.14.cloned.1.call-done) | copy-start | bytes 7077892
  452.5 20.1 %copy-start.11 = (f32[1024]{0:T(1024)S(1)}, f32[1024]{0:T(1024)}, u32[]{:S(2)}) copy-start(f32[1024]{0:T(1024)} %copy-done.10) | copy-start | bytes 12292
  452.5 38.8 %all-gather.20.cloned.1.call-start = ((), (), s32[]{:S(2)}) async-start(), calls=%async_computation.16 | async-start | bytes 4718592 | tf_op jit(solution)/shard_map/all_gather | solution.py:173
  474.1 3.7 copy-start.8
  475.7 15.6 %copy-start.7 = (bf16[384,768]{0,1:T(8,128)(2,1)S(1)}, bf16[384,768]{0,1:T(8,128)(2,1)}, u32[]{:S(2)}) copy-start(bf16[384,768]{0,1:T(8,128)(2,1)} %all_gather.26) | copy-start | bytes 1769476
  477.8 552.8 %all-reduce.4.cloned.1.call-start = ((), (), s32[]{:S(2)}) async-start(), calls=%async_computation.21 | async-start | bytes 9437184
  497.8 4.0 copy-start.27
  523.1 3.5 copy-start.1
  535.0 3.5 copy-start.1
  546.9 3.5 copy-start.1
  577.8 3.5 copy-start.1
  589.7 3.5 copy-start.1
  601.6 3.5 copy-start.1
  620.6 3.5 copy-start.1
  632.5 3.5 copy-start.1
  656.3 3.5 copy-start.1
  687.2 3.5 copy-start.1
  699.1 3.5 copy-start.1
  741.9 3.5 copy-start.1
  765.7 3.5 copy-start.1
  808.5 3.5 copy-start.1
  820.4 3.5 copy-start.1
  832.0 4.5 copy-start.28
  851.0 194.0 %reduce-scatter.14.cloned.1.call-start = ((), (), s32[]{:S(2)}) async-start(), calls=%async_computation.17 | async-start | bytes 4718592 | tf_op jit(solution)/shard_map/reduce_scatter | solution.py:204
  860.8 328.6 %reduce-scatter.20.cloned.1.call-start = ((), (), s32[]{:S(2)}) async-start(), calls=%async_computation.20 | async-start | bytes 5013504 | tf_op jit(solution)/shard_map/reduce_scatter | solution.py:200
  872.2 458.8 %reduce-scatter.18.cloned.1.call-start = ((), (), s32[]{:S(2)}) async-start(), calls=%async_computation.19 | async-start | bytes 5013504 | tf_op jit(solution)/shard_map/reduce_scatter | solution.py:199
  883.7 5.7 copy-start.25
  883.7 6.8 copy-start.16
  883.7 6.8 copy-start.15
  883.7 6.8 copy-start.14
  883.8 6.8 copy-start.18
  883.8 6.9 copy-start.17
  883.8 6.9 copy-start.13
  883.8 6.9 copy-start.12
  883.8 161.2 %copy-start.9 = (f32[1024]{0:T(1024)S(1)}, f32[1024]{0:T(1024)}, u32[]{:S(2)}) copy-start(f32[1024]{0:T(1024)} %copy-done.8) | copy-start | bytes 12292
  883.8 575.8 %reduce-scatter.16.cloned.1.call-start = ((), (), s32[]{:S(2)}) async-start(), calls=%async_computation.18 | async-start | bytes 1253376 | tf_op jit(solution)/shard_map/reduce_scatter | solution.py:198
  883.9 161.1 %copy-start.3 = (f32[1024,768]{1,0:T(8,128)S(1)}, f32[1024,768]{1,0:T(8,128)}, u32[]{:S(2)}) copy-start(f32[1024,768]{1,0:T(8,128)} %copy-done.2) | copy-start | bytes 9437188
  (43 other events, 96.6 us)
Sparse Core Ops, SparseCore 0:
  9.6 13.4 all-gather.9
  25.8 59.4 all-gather.7
  216.1 14.0 reduce-scatter.7
  233.3 63.5 all-gather.13
  298.9 10.7 all-gather.11
  312.8 63.5 all-gather.15
  386.2 13.1 reduce-scatter.9
  412.0 13.2 all-gather.17
  452.6 15.6 reduce-scatter.11
  478.0 13.2 all-gather.19
  851.1 179.5 all-reduce.3
  1033.4 11.5 reduce-scatter.13
  1051.5 137.7 reduce-scatter.19
  1195.0 136.0 reduce-scatter.17
  1336.9 122.6 reduce-scatter.15
where the time goes:
time: 1480 us; the launch traced here: 1470 us
  waiting for transfers between devices  735 us (50%)
  matrix products  341 us (23%)
  local copies, waits for them, and re-layouts  154 us (10%)
  other arithmetic  136 us (9%)
  blocking collectives  80.2 us (5%)
  between operations  15.8 us (1%)
    reduce_scatter x1, waiting for transfers between devices, body(): lax.psum_scatter(up_grad, 'dp', scatter_dimension=0, tiled=True)  142 us
    reduce_scatter x1, waiting for transfers between devices, body(): lax.psum_scatter(down_grad, 'dp', scatter_dimension=1, tiled=True)  141 us
    reduce_scatter x1, waiting for transfers between devices, body(): lax.psum_scatter(out_proj_grad, 'dp', scatter_dimension=1, tiled=True)  129 us
    unnamed x16, waiting for transfers between devices  99.2 us
    dot_general x24, matrix products, one_step(): jnp.einsum('qk,qd->kd', attn_probs.astype(jnp.bfloat16), ctx_block, prefe...  83 us
    all_gather x1, waiting for transfers between devices, body(): lax.all_gather(w_up, 'dp', axis=0, tiled=True)  60.4 us
    while x96, local copies, waits for them, and re-layouts  49 us
    psum x1, blocking collectives, body(): lax.psum((gain_grads, shift_grads, spread_bias), ('dp', 'tensor'))  42.6 us
  transfers between devices with their start and end apart: 15, of which 14 were waited for; matrix products, arithmetic and copies ran while one was open for 6% of the time, Pallas kernels for 0%

commit v1 on v0

--- a/solution.py
+++ b/solution.py
@@ -1,6 +1,8 @@
 import jax
 import jax.numpy as jnp
 from jax import lax
+from jax.experimental import pallas as pl
+from jax.experimental.pallas import tpu as pltpu
 from jax.sharding import PartitionSpec as P
 
 HD = 64
@@ -21,79 +23,167 @@
     return jax.nn.gelu(ff_pre, approximate=False)
 
 
-def softmax_rows(query_block, key_rows, key_mask):
-    scores = jnp.einsum("qd,kd->qk", query_block, key_rows, preferred_element_type=jnp.float32)
-    scores = jnp.where(key_mask[None, :], scores, masked_score)
-    row_max = jnp.max(scores, axis=-1, keepdims=True)
-    shifted = jnp.exp(scores - row_max)
-    return shifted / jnp.sum(shifted, axis=-1, keepdims=True)
-
-
-def heads_first(matrix, seq_count, head_count):
-    return (
-        matrix.reshape(seq_count, LEN, head_count, HD)
-        .transpose(0, 2, 1, 3)
-        .reshape(seq_count * head_count, LEN, HD)
-    )
-
-
-def heads_last(stacked, seq_count, head_count):
-    return (
-        stacked.reshape(seq_count, head_count, LEN, HD)
-        .transpose(0, 2, 1, 3)
-        .reshape(seq_count * LEN, head_count * HD)
-    )
-
-
-def attend_forward(member):
-    query_rows, key_rows, value_rows, seq_len = member
-    key_mask = jnp.arange(LEN, dtype=jnp.int32) < seq_len
-    block_rows = min(512, LEN)
-
-    def one_block(query_block):
-        attn_probs = softmax_rows(query_block, key_rows, key_mask)
-        return jnp.dot(
-            attn_probs.astype(jnp.bfloat16), value_rows, preferred_element_type=jnp.float32
-        )
-
-    context = lax.map(one_block, query_rows.reshape(LEN // block_rows, block_rows, HD))
-    return context.reshape(LEN, HD)
-
-
-def attend_backward(member):
-    query_rows, key_rows, value_rows, ctx_rows, seq_len = member
-    key_mask = jnp.arange(LEN, dtype=jnp.int32) < seq_len
-    block_rows = min(512, LEN)
-
-    def one_step(totals, blocks):
-        key_total, value_total = totals
-        query_block, ctx_block = blocks
-        attn_probs = softmax_rows(query_block, key_rows, key_mask)
-        prob_grad = jnp.einsum(
-            "qd,kd->qk", ctx_block, value_rows, preferred_element_type=jnp.float32
-        )
-        delta = jnp.sum(attn_probs * prob_grad, axis=-1, keepdims=True)
-        score_grad = (attn_probs * (prob_grad - delta)).astype(jnp.bfloat16)
-        query_part = jnp.einsum(
-            "qk,kd->qd", score_grad, key_rows, preferred_element_type=jnp.float32
-        )
-        key_total = key_total + jnp.einsum(
-            "qk,qd->kd", score_grad, query_block, preferred_element_type=jnp.float32
-        )
-        value_total = value_total + jnp.einsum(
-            "qk,qd->kd",
-            attn_probs.astype(jnp.bfloat16),
-            ctx_block,
-            preferred_element_type=jnp.float32,
-        )
-        return ((key_total, value_total), query_part)
-
-    zeros_init = jnp.zeros((LEN, HD), jnp.float32)
-    shaped = (LEN // block_rows, block_rows, HD)
-    (key_grad, value_grad), query_grad = lax.scan(
-        one_step, (zeros_init, zeros_init), (query_rows.reshape(shaped), ctx_rows.reshape(shaped))
-    )
-    return (query_grad.reshape(LEN, HD), key_grad, value_grad)
+PAIR = 2 * HD
+QUERY_ROWS = 512
+KEY_ROWS = 512
+
+
+def split_heads(rows):
+    lane = lax.broadcasted_iota(jnp.int32, rows.shape, 1)
+    blank = jnp.zeros_like(rows)
+    return (jnp.where(lane < HD, rows, blank), jnp.where(lane < HD, blank, rows))
+
+
+def dot_nt(left, right):
+    return lax.dot_general(
+        left, right, (((1,), (1,)), ((), ())), preferred_element_type=jnp.float32
+    )
+
+
+def dot_nn(left, right):
+    return jnp.dot(left, right, preferred_element_type=jnp.float32)
+
+
+def masked_scores(key_block, query_head, chunk, seq_len):
+    scores = dot_nt(key_block, query_head)
+    if (chunk + 1) * KEY_ROWS > LEN // 2:
+        place = lax.broadcasted_iota(jnp.int32, scores.shape, 0) + chunk * KEY_ROWS
+        scores = jnp.where(place < seq_len, scores, masked_score)
+    return scores
+
+
+def forward_kernel(lens_ref, q_ref, k_ref, vt_ref, ctx_ref, lse_ref):
+    seq_len = lens_ref[pl.program_id(0)]
+    parts = []
+    for head, query_head in enumerate(split_heads(q_ref[...])):
+        rows = pl.ds(head * HD, HD)
+        blocks = [
+            masked_scores(k_ref[pl.ds(c * KEY_ROWS, KEY_ROWS), :], query_head, c, seq_len)
+            for c in range(LEN // KEY_ROWS)
+        ]
+        tops = [jnp.max(block, axis=0, keepdims=True) for block in blocks]
+        top = tops[0]
+        for other in tops[1:]:
+            top = jnp.maximum(top, other)
+        total = jnp.zeros_like(top)
+        context = jnp.zeros((HD, QUERY_ROWS), jnp.float32)
+        for c, block in enumerate(blocks):
+            shifted = jnp.exp(block - top)
+            total = total + jnp.sum(shifted, axis=0, keepdims=True)
+            context = context + dot_nn(
+                vt_ref[rows, pl.ds(c * KEY_ROWS, KEY_ROWS)], shifted.astype(jnp.bfloat16)
+            )
+        parts.append(context / total)
+        lse_ref[0, 0, pl.ds(head, 1), :] = top + jnp.log(total)
+    ctx_ref[...] = jnp.concatenate(parts, axis=0).T.astype(jnp.bfloat16)
+
+
+def backward_kernel(
+    lens_ref, q_ref, k_ref, kt_ref, v_ref, ctx_ref, grad_ref, lse_ref,
+    dq_ref, dk_ref, dv_ref, key_sum, value_sum,
+):
+    seq_len = lens_ref[pl.program_id(0)]
+    step = pl.program_id(2)
+
+    @pl.when(step == 0)
+    def _():
+        key_sum[...] = jnp.zeros_like(key_sum)
+        value_sum[...] = jnp.zeros_like(value_sum)
+
+    product = (grad_ref[...].astype(jnp.float32) * ctx_ref[...].astype(jnp.float32)).T
+    deltas = [
+        jnp.sum(product[h * HD : (h + 1) * HD], axis=0, keepdims=True) for h in range(2)
+    ]
+    query_heads = split_heads(q_ref[...])
+    grad_heads = split_heads(grad_ref[...])
+    query_grads = [jnp.zeros((HD, QUERY_ROWS), jnp.float32) for _ in range(2)]
+    for c in range(LEN // KEY_ROWS):
+        span = pl.ds(c * KEY_ROWS, KEY_ROWS)
+        key_add = None
+        value_add = None
+        for head in range(2):
+            scores = masked_scores(k_ref[span, :], query_heads[head], c, seq_len)
+            probs = jnp.exp(scores - lse_ref[0, 0, pl.ds(head, 1), :])
+            prob_grad = dot_nt(v_ref[span, :], grad_heads[head])
+            score_grad = (probs * (prob_grad - deltas[head])).astype(jnp.bfloat16)
+            value_part = dot_nn(probs.astype(jnp.bfloat16), grad_heads[head])
+            key_part = dot_nn(score_grad, query_heads[head])
+            value_add = value_part if head == 0 else value_add + value_part
+            key_add = key_part if head == 0 else key_add + key_part
+            query_grads[head] = query_grads[head] + dot_nn(
+                kt_ref[pl.ds(head * HD, HD), span], score_grad
+            )
+        key_sum[span, :] += key_add
+        value_sum[span, :] += value_add
+    query_grad = jnp.concatenate(query_grads, axis=0).T.astype(jnp.bfloat16)
+    dq_ref[...] = (query_grad.astype(jnp.float32) * HD ** (-0.5)).astype(jnp.bfloat16)
+
+    @pl.when(step == pl.num_programs(2) - 1)
+    def _():
+        dk_ref[...] = key_sum[...].astype(jnp.bfloat16)
+        dv_ref[...] = value_sum[...].astype(jnp.bfloat16)
+
+
+def attention_specs():
+    blocks = LEN // QUERY_ROWS
+    lens = pl.BlockSpec(memory_space=pltpu.SMEM)
+    query = pl.BlockSpec((QUERY_ROWS, PAIR), lambda s, p, i: (s * blocks + i, p))
+    whole = pl.BlockSpec((LEN, PAIR), lambda s, p, i: (s, p))
+    turned = pl.BlockSpec((PAIR, LEN), lambda s, p, i: (p, s))
+    lse = pl.BlockSpec((1, 1, 2, QUERY_ROWS), lambda s, p, i: (s, p, 0, i))
+    return lens, query, whole, turned, lse
+
+
+def attend(lengths, queries, keys_all, values_turned):
+    seqs, pairs = lengths.shape[0], queries.shape[1] // PAIR
+    lens, query, whole, turned, lse = attention_specs()
+    return pl.pallas_call(
+        forward_kernel,
+        grid=(seqs, pairs, LEN // QUERY_ROWS),
+        in_specs=[lens, query, whole, turned],
+        out_specs=[query, lse],
+        out_shape=[
+            jax.ShapeDtypeStruct(queries.shape, jnp.bfloat16),
+            jax.ShapeDtypeStruct((seqs, pairs, 2, LEN), jnp.float32),
+        ],
+        compiler_params=pltpu.CompilerParams(vmem_limit_bytes=56 * 1024 * 1024),
+        name="attend_forward",
+    )(lengths, queries, keys_all, values_turned)
+
+
+def attend_back(lengths, queries, keys_all, keys_turned, values_all, context, context_grad, stats):
+    seqs, pairs = lengths.shape[0], queries.shape[1] // PAIR
+    lens, query, whole, turned, lse = attention_specs()
+    shape = jax.ShapeDtypeStruct(queries.shape, jnp.bfloat16)
+    return pl.pallas_call(
+        backward_kernel,
+        grid=(seqs, pairs, LEN // QUERY_ROWS),
+        in_specs=[lens, query, whole, turned, whole, query, query, lse],
+        out_specs=[query, whole, whole],
+        out_shape=[shape, shape, shape],
+        scratch_shapes=[pltpu.VMEM((LEN, PAIR), jnp.float32)] * 2,
+        compiler_params=pltpu.CompilerParams(vmem_limit_bytes=56 * 1024 * 1024),
+        name="attend_backward",
+    )(lengths, queries, keys_all, keys_turned, values_all, context, context_grad, stats)
+
+
+def owned_parts(*grads):
+    count = lax.axis_size("dp")
+    pieces, shapes = [], []
+    for grad, dim in grads:
+        cut = grad.shape[:dim] + (count, grad.shape[dim] // count) + grad.shape[dim + 1 :]
+        piece = jnp.moveaxis(grad.astype(jnp.bfloat16).reshape(cut), dim, 0)
+        shapes.append(piece.shape[1:])
+        pieces.append(piece.reshape(count, -1, 128))
+    sent = lax.all_to_all(
+        jnp.concatenate(pieces, axis=1), "dp", split_axis=0, concat_axis=0, tiled=True
+    )
+    summed = jnp.sum(sent.astype(jnp.float32), axis=0)
+    owned, start = [], 0
+    for piece, shape in zip(pieces, shapes):
+        owned.append(summed[start : start + piece.shape[1]].reshape(shape))
+        start += piece.shape[1]
+    return owned
 
 
 def body(inputs, out_grad, lengths, w_qkv, w_out, w_up, w_down, gains, shifts, ff_bias):
@@ -112,12 +202,7 @@
     queries = (projected[0] * score_scale).astype(jnp.bfloat16)
     keys_all = projected[1].astype(jnp.bfloat16)
     values_all = projected[2].astype(jnp.bfloat16)
-    head_lens = jnp.repeat(lengths, head_count)
-    query_heads = heads_first(queries, seq_count, head_count)
-    key_heads = heads_first(keys_all, seq_count, head_count)
-    value_heads = heads_first(values_all, seq_count, head_count)
-    context_f = lax.map(attend_forward, (query_heads, key_heads, value_heads, head_lens))
-    context = heads_last(context_f, seq_count, head_count).astype(jnp.bfloat16)
+    context, stats = attend(lengths, queries, keys_all, values_all.T)
     attn_branch = (
         lax.psum_scatter(
             jnp.dot(context, out_full, preferred_element_type=jnp.float32),
@@ -177,32 +262,20 @@
     out_proj_grad = jnp.einsum(
         "re,rd->ed", context, attn_grad_all, preferred_element_type=jnp.float32
     )
-    ctx_heads = heads_first(context_grad, seq_count, head_count)
-    query_grad, key_grad, value_grad = lax.map(
-        attend_backward, (query_heads, key_heads, value_heads, ctx_heads, head_lens)
+    down_owned, up_owned, out_owned = owned_parts(
+        (down_grad, 1), (up_grad, 0), (out_proj_grad, 1)
     )
     stacked_grad = jnp.stack(
-        [
-            heads_last(query_grad, seq_count, head_count),
-            heads_last(key_grad, seq_count, head_count),
-            heads_last(value_grad, seq_count, head_count),
-        ]
-    ).astype(jnp.bfloat16)
-    qkv_scale = jnp.array([score_scale, 1.0, 1.0], jnp.float32)
-    qkv_grad = (
-        jnp.einsum("rd,cre->cde", gathered, stacked_grad, preferred_element_type=jnp.float32)
-        * qkv_scale[:, None, None]
-    )
-    qkv_owned, out_owned, up_owned, down_owned = (
-        lax.psum_scatter(qkv_grad, "dp", scatter_dimension=1, tiled=True),
-        lax.psum_scatter(out_proj_grad, "dp", scatter_dimension=1, tiled=True),
-        lax.psum_scatter(up_grad, "dp", scatter_dimension=0, tiled=True),
-        lax.psum_scatter(down_grad, "dp", scatter_dimension=1, tiled=True),
-    )
+        attend_back(
+            lengths, queries, keys_all, keys_all.T, values_all, context, context_grad, stats
+        )
+    )
+    qkv_grad = jnp.einsum("rd,cre->cde", gathered, stacked_grad, preferred_element_type=jnp.float32)
+    (qkv_owned,) = owned_parts((qkv_grad, 1))
     slab_rows = stacked_grad
-    parts = jnp.einsum("cre,cde->crd", slab_rows, qkv_full, preferred_element_type=jnp.float32)
+    parts = jnp.einsum("cre,cde->rd", slab_rows, qkv_full, preferred_element_type=jnp.float32)
     input_grad = resid_one_grad + lax.psum_scatter(
-        (parts[0] * score_scale + parts[1] + parts[2]).astype(jnp.bfloat16),
+        parts.astype(jnp.bfloat16),
         "tensor",
         scatter_dimension=0,
         tiled=True,

time: 1480 us -> 751 us (0.51)
  waiting for transfers between devices: 735 us -> 216 us
  matrix products: 341 us -> 123 us
  Pallas kernels: 0 us -> 119 us
  local copies, waits for them, and re-layouts: 154 us -> 48 us
  other arithmetic: 136 us -> 37.2 us
  blocking collectives: 80.2 us -> 165 us
    reduce_scatter x4 -> x1, waiting for transfers between devices: 424 us -> 0.01 us  [body(): lax.psum_scatter(parts.astype(jnp.bfloat16), 'tensor', scatter_dimension=...]
    dot_general x169 -> x1, matrix products: 220 us -> 7.91 us  [body(): jnp.einsum('cre,cde->rd', slab_rows, qkv_full, preferred_element_type=jnp...]
    pallas_call x0 -> x2, Pallas kernels: none -> 119 us  [the longest x1 73.6 us: attend_back(): pl.pallas_call(backward_kernel, grid=(seqs, pairs, LEN // QUERY_ROWS), in...]
    unnamed x16 -> x11, waiting for transfers between devices: 99.2 us -> 2.54 us
    psum x1, blocking collectives: 42.6 us -> 131 us  [body(): lax.psum((gain_grads, shift_grads, spread_bias), ('dp', 'tensor'))]
    while x108 -> x0, local copies, waits for them, and re-layouts: 52.3 us -> none
    convert_element_type x25 -> x0, other arithmetic: 36.7 us -> none  [the longest x24 34.2 us: one_step(): score_grad = (attn_probs * (prob_grad - delta)).astype(jnp.bfloat16)]
    reduce_sum x48 -> x2, other arithmetic: 39.2 us -> 5.04 us  [owned_parts(): summed = jnp.sum(sent.astype(jnp.float32), axis=0)]
  transfers between devices with their start and end apart: 15 -> 13, of which waited for: 14 -> 9; matrix products, arithmetic and copies ran while one was open for 6% -> 15% of each run, Pallas kernels for 0% -> 0%
where the time goes in v1:
time: 751 us; the launch traced here: 740 us
  waiting for transfers between devices  216 us (29%)
  blocking collectives  165 us (22%)
  matrix products  123 us (16%)
  Pallas kernels  119 us (16%)
  local copies, waits for them, and re-layouts  48 us (6%)
  other arithmetic  37.2 us (5%)
  starting transfers between devices  16.2 us (2%)
  between operations  15.4 us (2%)
    psum x1, blocking collectives, body(): lax.psum((gain_grads, shift_grads, spread_bias), ('dp', 'tensor'))  131 us
    pallas_call x1, Pallas kernels, attend_back(): pl.pallas_call(backward_kernel, grid=(seqs, pairs, LEN // QUERY_ROWS), in...  73.6 us
    all_gather x1, waiting for transfers between devices, body(): lax.all_gather(w_up, 'dp', axis=0, tiled=True)  60.4 us
    pallas_call x1, Pallas kernels, attend(): pl.pallas_call(forward_kernel, grid=(seqs, pairs, LEN // QUERY_ROWS), in_...  45.7 us
    all_gather x1, waiting for transfers between devices, body(): lax.all_gather(w_qkv, 'dp', axis=1, tiled=True)  41.5 us
    dot_general x1, matrix products, body(): jnp.dot(normed_all, up_full, preferred_element_type=jnp.float32)  34.9 us
    all_gather x1, blocking collectives, body(): lax.all_gather(w_out, 'dp', axis=1, tiled=True)  34.5 us
    all_gather x1, waiting for transfers between devices, body(): lax.all_gather(w_down, 'dp', axis=1, tiled=True)  31.8 us
  transfers between devices with their start and end apart: 13, of which 9 were waited for; matrix products, arithmetic and copies ran while one was open for 15% of the time, Pallas kernels for 0%

profile of v1, /device:TPU:12, one launch (start us, length us, event | category | flops | bytes accessed | tf_op | source)
XLA Modules:
  0.0 740.3 jit_solution(18107805731335163195)
XLA Ops:
  9.4 34.5 %all_gather.26 = bf16[384,768]{0,1:T(8,128)(2,1)S(1)} all-gather(bf16[384,48]{0,1:T(8,128)(2,1)} %param.14), channel_id=1, replica_groups=mesh['dp'=16,'tensor'=2] {'dp'}, dimensions={1}, use_global_device_ids=true | all-gather | bytes 626688 | tf_op jit(solution)/shard_map/all_gather | solution.py:199
  43.9 41.5 %all-gather.8.cloned.1.call-done = bf16[3,768,384]{2,1,0:T(8,128)(2,1)} async-done(((bf16[3,48,384]{2,1,0:T(8,128)(2,1)}), bf16[3,768,384]{2,1,0:T(8,128)(2,1)}) %all-gather.8.cloned.1.call-update) | async-done | bytes 1769488 | tf_op jit(solution)/shard_map/all_gather | solution.py:198
  85.4 6.8 fusion.27
  93.6 2.4 slice_bitcast_fusion.1
  97.5 45.7 %attend_forward.1 = (bf16[2048,384]{1,0:T(8,128)(2,1)}, f32[1,3,2,2048]{3,2,1,0:T(2,128)}) custom-call(s32[1]{0:T(128)S(6)} %copy.48.lens_ref, bf16[2048,384]{1,0:T(8,128)(2,1)} %fusion.16.q_ref, bf16[2048,384]{1,0:T(8,128)(2,1)} %get-tuple-element.70.k_ref, bf16[384,2048]{1,0:T(8,128)(2,1)} %copy.36.vt_ref), custom_call_target="tpu_custom_call" | custom-call | tf_op jit(solution)/shard_map/attend_forward/pallas_call | solution.py:140
  143.3 5.9 fusion.28
  150.1 13.3 %reduce-scatter.5.cloned.1.call-done = f32[1024,768]{1,0:T(8,128)} async-done(((f32[2048,768]{1,0:T(8,128)}), f32[1024,768]{1,0:T(8,128)}) %reduce-scatter.5.cloned.1.call-update) | async-done | bytes 3145744 | tf_op jit(solution)/shard_map/reduce_scatter | solution.py:207
  163.4 2.8 fusion.25
  167.4 1.7 add_convert_fusion.2
  169.7 60.4 %all-gather.14.cloned.1.call-done = bf16[768,1536]{1,0:T(8,128)(2,1)} async-done(((bf16[48,1536]{1,0:T(8,128)(2,1)}), bf16[768,1536]{1,0:T(8,128)(2,1)}) %all-gather.14.cloned.1.call-update) | async-done | bytes 2359312 | tf_op jit(solution)/shard_map/all_gather | solution.py:220
  230.1 12.9 %all-gather.12.cloned.1.call-done = bf16[2048,768]{1,0:T(8,128)(2,1)} async-done(((bf16[1024,768]{1,0:T(8,128)(2,1)}), bf16[2048,768]{1,0:T(8,128)(2,1)}) %all-gather.12.cloned.1.call-update) | async-done | bytes 3145744 | tf_op jit(solution)/shard_map/all_gather | solution.py:218
  243.0 34.9 %multiply_convert_fusion = (bf16[2048,1536]{1,0:T(8,128)(2,1)}, f32[2048,1536]{1,0:T(8,128)}, f32[2048,1536]{1,0:T(8,128)}) fusion(f32[1536]{0:T(1024)S(1)} %convert_element_type.102, bf16[2048,768]{1,0:T(8,128)(2,1)} %all-gather.12.cloned.1.call-done, bf16[768,1536]{1,0:T(8,128)(2,1)} %all-gather.14.cloned.1.call-done), kind=kOutput, calls=%fused_computation.4 | convolution fusion | flops 5039456256 | bytes 36968448 | tf_op jit(solution)/shard_map/dot_general | solution.py:223
  277.8 31.8 %all-gather.16.cloned.1.call-done = bf16[1536,768]{0,1:T(8,128)(2,1)} async-done(((bf16[1536,48]{0,1:T(8,128)(2,1)}), bf16[1536,768]{0,1:T(8,128)(2,1)}) %all-gather.16.cloned.1.call-update) | async-done | bytes 2359312 | tf_op jit(solution)/shard_map/all_gather | solution.py:221
  309.7 9.6 %fusion.29 = f32[2048,768]{1,0:T(8,128)} fusion(bf16[2048,1536]{1,0:T(8,128)(2,1)} %get-tuple-element.63, bf16[1536,768]{0,1:T(8,128)(2,1)} %all-gather.16.cloned.1.call-done), kind=kOutput, calls=%fused_computation.92 | convolution fusion | flops 4831838208 | bytes 14942208 | tf_op jit(solution)/shard_map/dot_general | solution.py:230
  319.8 12.9 %reduce-scatter.7.cloned.1.call-done = f32[1024,768]{1,0:T(8,128)} async-done(((f32[2048,768]{1,0:T(8,128)}), f32[1024,768]{1,0:T(8,128)}) %reduce-scatter.7.cloned.1.call-update) | async-done | bytes 3145744 | tf_op jit(solution)/shard_map/reduce_scatter | solution.py:229
  332.6 2.9 fusion.23
  336.9 1.8 fusion.9
  338.8 2.6 fusion.22
  341.3 1.7 copy-done.2
  343.0 2.1 convert_reduce_fusion.4
  345.2 13.4 %all-gather.18.cloned.1.call-done = bf16[2048,768]{1,0:T(8,128)(2,1)} async-done(((bf16[1024,768]{1,0:T(8,128)(2,1)}), bf16[2048,768]{1,0:T(8,128)(2,1)}) %all-gather.18.cloned.1.call-update) | async-done | bytes 3145744 | tf_op jit(solution)/shard_map/all_gather | solution.py:242
  358.6 17.6 %convert_reduce_fusion = (f32[1536]{0:T(1024)}, bf16[2048,1536]{1,0:T(8,128)(2,1)S(1)}) fusion(f32[2048,1536]{1,0:T(8,128)} %get-tuple-element.64, bf16[2048,768]{1,0:T(8,128)(2,1)} %all-gather.18.cloned.1.call-done, bf16[1536,768]{0,1:T(8,128)(2,1)} %all-gather.16.cloned.1.call-done, f32[2048,1536]{1,0:T(8,128)} %get-tuple-element.76, ...), kind=kOutput, calls=%fused_computation.2 | convolution fusion | flops 4885314048 | bytes 36974592 | tf_op jit(solution)/shard_map/rd,fd->rf/dot_general | solution.py:243
  376.2 2.7 copy-done.21
  378.8 6.9 fusion.30
  386.0 15.6 %reduce-scatter.9.cloned.1.call-done = f32[1024,768]{1,0:T(8,128)} async-done(((f32[2048,768]{1,0:T(8,128)}), f32[1024,768]{1,0:T(8,128)}) %reduce-scatter.9.cloned.1.call-update) | async-done | bytes 3145744 | tf_op jit(solution)/shard_map/reduce_scatter | solution.py:249
  401.5 3.7 multiply_reduce_fusion
  408.4 2.0 convert_reduce_fusion.5
  410.5 1.6 copy.37.kt_ref
  412.1 11.8 %all-gather.20.cloned.1.call-done = bf16[2048,768]{1,0:T(8,128)(2,1)} async-done(((bf16[1024,768]{1,0:T(8,128)(2,1)}), bf16[2048,768]{1,0:T(8,128)(2,1)}) %all-gather.20.cloned.1.call-update) | async-done | bytes 3145744 | tf_op jit(solution)/shard_map/all_gather | solution.py:258
  423.9 4.8 convolution_convert_fusion.2.grad_ref
  428.7 73.6 %attend_backward.1 = (bf16[2048,384]{1,0:T(8,128)(2,1)}, bf16[2048,384]{1,0:T(8,128)(2,1)}, bf16[2048,384]{1,0:T(8,128)(2,1)}) custom-call(s32[1]{0:T(128)S(6)} %copy.48.lens_ref, bf16[2048,384]{1,0:T(8,128)(2,1)} %fusion.16.q_ref, bf16[2048,384]{1,0:T(8,128)(2,1)} %get-tuple-element.70.k_ref, bf16[384,2048]{1,0:T(8,128)(2,1)} %copy.37.kt_ref, ...), custom_call_target="tpu_custom_call" | custom-call | tf_op jit(solution)/shard_map/attend_backward/pallas_call | solution.py:158
  502.3 6.3 convert_bitcast_fusion
  509.9 2.2 reshape.129
  512.1 7.6 %all-to-all-start = ((bf16[16,432,128]{2,1,0:T(8,128)(2,1)}), bf16[16,432,128]{2,1,0:T(8,128)(2,1)}, u32[]{:S(2)}, u32[]{:S(2)}) async-start(bf16[16,432,128]{2,1,0:T(8,128)(2,1)} %reshape.129), calls=%async_computation.4 | async-start | bytes 3538944 | tf_op jit(solution)/shard_map/all_to_all | solution.py:178
  519.7 9.1 %convolution_convert_fusion = bf16[768,1536]{1,0:T(8,128)(2,1)} fusion(bf16[2048,768]{1,0:T(8,128)(2,1)S(1)} %copy-done.17, bf16[2048,1536]{1,0:T(8,128)(2,1)} %copy-done.21), kind=kOutput, calls=%fused_computation.31 | convolution fusion | flops 4833017856 | bytes 11796480 | tf_op jit(solution)/shard_map/rd,rf->df/dot_general | solution.py:247
  528.8 4.6 reshape_reshape.3
  533.4 9.6 %convolution_convert_fusion.1 = bf16[1536,768]{0,1:T(8,128)(2,1)} fusion(bf16[2048,1536]{1,0:T(8,128)(2,1)} %get-tuple-element.63, bf16[2048,768]{1,0:T(8,128)(2,1)} %all-gather.18.cloned.1.call-done), kind=kOutput, calls=%fused_computation.32 | convolution fusion | flops 4833017856 | bytes 11796480 | tf_op jit(solution)/shard_map/rf,rd->fd/dot_general | solution.py:244
  543.0 6.4 copy.41
  549.5 10.9 %reshape.132 = bf16[16,576,128]{2,1,0:T(8,128)(2,1)} reshape(bf16[16,1536,48]{2,1,0:T(8,128)(2,1)} %bitcast.60) | data formatting | bytes 4718592 | tf_op jit(solution)/shard_map/reshape | solution.py:177
  560.4 3.8 convolution_convert_fusion.3
  566.0 3.3 reshape.134
  569.3 4.3 pad_maximum_fusion
  573.7 7.2 all-to-all-start.1
  581.2 7.9 %bitcast_convert_fusion = bf16[2048,768]{1,0:T(8,128)(2,1)} fusion(bf16[3,768,384]{2,1,0:T(8,128)(2,1)S(1)} %copy-done.19, bf16[1,2048,384]{2,1,0:T(8,128)(2,1)} %bitcast.69, bf16[1,2048,384]{2,1,0:T(8,128)(2,1)} %bitcast.67, bf16[1,2048,384]{2,1,0:T(8,128)(2,1)S(1)} %bitcast.65), kind=kOutput, calls=%fused_computation.19 | convolution fusion | flops 3630170112 | bytes 9633792 | tf_op jit(solution)/shard_map/cre,cde->rd/dot_general | solution.py:276
  590.0 130.5 %all-reduce = (f32[2,768]{1,0:T(2,128)}, f32[4,768]{1,0:T(4,128)}, f32[2,1536]{1,0:T(2,128)S(1)}) all-reduce(f32[2,768]{1,0:T(2,128)S(1)} %pad_maximum_fusion.7, f32[4,768]{1,0:T(4,128)S(1)} %pad_maximum_fusion.6, f32[2,1536]{1,0:T(2,128)S(1)} %broadcast_multiply_fusion), channel_id=1, replica_groups=mesh['dp'=16,'tensor'=2] {'dp','tensor'}, use_global_device_ids=true, to_apply=%region_16.0 | all-reduce | flops 7680 | bytes 61440 | tf_op jit(solution)/shard_map/psum | solution.py:290
  721.2 1.7 convert_reduce_fusion.3
  723.7 3.4 convert_add_fusion
  727.1 3.3 convert_reduce_fusion.1
  (109 shorter events, 21.0 us)
Async XLA Ops:
  7.2 36.7 %all-gather.10.cloned.1.call-start = ((), (), s32[]{:S(2)}) async-start(), calls=%async_computation.7 | async-start | bytes 4718592 | tf_op jit(solution)/shard_map/all_gather | solution.py:196
  7.9 77.5 %all-gather.8.cloned.1.call-start = ((), (), s32[]{:S(2)}) async-start(), calls=%async_computation.6 | async-start | bytes 1880064 | tf_op jit(solution)/shard_map/all_gather | solution.py:198
  8.7 154.8 %reduce-scatter.5.cloned.1.call-start = ((), (), s32[]{:S(2)}) async-start(), calls=%async_computation.8 | async-start | bytes 9437184 | tf_op jit(solution)/shard_map/reduce_scatter | solution.py:207
  43.9 99.4 %copy-start.5 = (bf16[384,768]{0,1:T(8,128)(2,1)}, bf16[384,768]{0,1:T(8,128)(2,1)S(1)}, u32[]{:S(2)}) copy-start(bf16[384,768]{0,1:T(8,128)(2,1)S(1)} %all_gather.26) | copy-start | bytes 1769476
  149.2 0.9 copy-start.15
  149.2 0.9 copy-start.13
  149.2 80.9 %all-gather.14.cloned.1.call-start = ((), (), s32[]{:S(2)}) async-start(), calls=%async_computation.10 | async-start | bytes 2506752 | tf_op jit(solution)/shard_map/all_gather | solution.py:220
  149.8 93.2 %all-gather.12.cloned.1.call-start = ((), (), s32[]{:S(2)}) async-start(), calls=%async_computation.9 | async-start | bytes 4718592 | tf_op jit(solution)/shard_map/all_gather | solution.py:218
  166.8 0.6 copy-start.7
  167.4 2.4 copy-start.14
  169.1 140.6 %all-gather.16.cloned.1.call-start = ((), (), s32[]{:S(2)}) async-start(), calls=%async_computation.11 | async-start | bytes 2506752 | tf_op jit(solution)/shard_map/all_gather | solution.py:221
  169.7 162.9 %reduce-scatter.7.cloned.1.call-start = ((), (), s32[]{:S(2)}) async-start(), calls=%async_computation.12 | async-start | bytes 9437184 | tf_op jit(solution)/shard_map/reduce_scatter | solution.py:229
  319.3 39.3 %all-gather.18.cloned.1.call-start = ((), (), s32[]{:S(2)}) async-start(), calls=%async_computation.13 | async-start | bytes 4718592 | tf_op jit(solution)/shard_map/all_gather | solution.py:242
  335.5 1.4 copy-start.4
  341.3 1.7 copy-start.2
  345.1 56.4 %reduce-scatter.9.cloned.1.call-start = ((), (), s32[]{:S(2)}) async-start(), calls=%async_computation.14 | async-start | bytes 9437184 | tf_op jit(solution)/shard_map/reduce_scatter | solution.py:249
  358.6 20.2 %copy-start.18 = (bf16[768,1536]{1,0:T(8,128)(2,1)S(1)}, bf16[768,1536]{1,0:T(8,128)(2,1)}, u32[]{:S(2)}) copy-start(bf16[768,1536]{1,0:T(8,128)(2,1)} %all-gather.14.cloned.1.call-done) | copy-start | bytes 7077892
  376.1 2.7 copy-start.21
  385.7 19.5 %copy-start.8 = (f32[1024]{0:T(1024)S(1)}, f32[1024]{0:T(1024)}, u32[]{:S(2)}) copy-start(f32[1024]{0:T(1024)} %copy-done.7) | copy-start | bytes 12292
  385.7 38.2 %all-gather.20.cloned.1.call-start = ((), (), s32[]{:S(2)}) async-start(), calls=%async_computation.15 | async-start | bytes 4718592 | tf_op jit(solution)/shard_map/all_gather | solution.py:258
  406.7 1.6 copy-start
  408.4 2.1 copy-start.3
  410.4 13.5 %copy-start.6 = (bf16[384,768]{0,1:T(8,128)(2,1)S(1)}, bf16[384,768]{0,1:T(8,128)(2,1)}, u32[]{:S(2)}) copy-start(bf16[384,768]{0,1:T(8,128)(2,1)} %copy-done.5) | copy-start | bytes 1769476
  428.7 73.6 %copy-start.16 = (bf16[2048,768]{1,0:T(8,128)(2,1)S(1)}, bf16[2048,768]{1,0:T(8,128)(2,1)}, u32[]{:S(2)}) copy-start(bf16[2048,768]{1,0:T(8,128)(2,1)} %all-gather.10.cloned.1.call-done) | copy-start | bytes 9437188
  512.1 7.6 %copy-start.17 = (bf16[2048,768]{1,0:T(8,128)(2,1)S(1)}, bf16[2048,768]{1,0:T(8,128)(2,1)}, u32[]{:S(2)}) copy-start(bf16[2048,768]{1,0:T(8,128)(2,1)} %all-gather.12.cloned.1.call-done) | copy-start | bytes 9437188
  512.1 61.6 %all-to-all-start = ((bf16[16,432,128]{2,1,0:T(8,128)(2,1)}), bf16[16,432,128]{2,1,0:T(8,128)(2,1)}, u32[]{:S(2)}, u32[]{:S(2)}) async-start(bf16[16,432,128]{2,1,0:T(8,128)(2,1)} %reshape.129), calls=%async_computation.4 | async-start | bytes 3538944 | tf_op jit(solution)/shard_map/all_to_all | solution.py:178
  573.7 7.5 %copy-start.19 = (bf16[3,768,384]{2,1,0:T(8,128)(2,1)S(1)}, bf16[3,768,384]{2,1,0:T(8,128)(2,1)}, u32[]{:S(2)}) copy-start(bf16[3,768,384]{2,1,0:T(8,128)(2,1)} %all-gather.8.cloned.1.call-done) | copy-start | bytes 5308420
  573.7 7.5 %copy-start.20 = (bf16[2048,384]{1,0:T(8,128)(2,1)S(1)}, bf16[2048,384]{1,0:T(8,128)(2,1)}, u32[]{:S(2)}) copy-start(bf16[2048,384]{1,0:T(8,128)(2,1)} %get-tuple-element.16) | copy-start | bytes 4718596
  573.7 153.4 %all-to-all-start.1 = ((bf16[16,1296,128]{2,1,0:T(8,128)(2,1)}), bf16[16,1296,128]{2,1,0:T(8,128)(2,1)}, u32[]{:S(2)}, u32[]{:S(2)}) async-start(bf16[16,1296,128]{2,1,0:T(8,128)(2,1)} %pad_maximum_fusion), calls=%async_computation.5 | async-start | bytes 10616832 | tf_op jit(solution)/shard_map/all_to_all | solution.py:178
  580.8 142.8 %reduce-scatter.11.cloned.1.call-start = ((), (), s32[]{:S(2)}) async-start(), calls=%async_computation.16 | async-start | bytes 4718592 | tf_op jit(solution)/shard_map/reduce_scatter | solution.py:277
  589.1 0.7 copy-start.9
  589.1 0.7 copy-start.10
  589.1 0.7 copy-start.12
  589.1 0.8 copy-start.11
  589.1 134.6 %copy-start.1 = (f32[1024,768]{1,0:T(8,128)S(1)}, f32[1024,768]{1,0:T(8,128)}, u32[]{:S(2)}) copy-start(f32[1024,768]{1,0:T(8,128)} %copy-done) | copy-start | bytes 9437188
Sparse Core Ops, SparseCore 0:
  9.6 13.4 all-gather.9
  25.8 59.5 all-gather.7
  149.3 14.0 reduce-scatter.4
  166.5 63.5 all-gather.13
  232.1 10.7 all-gather.11
  246.0 63.6 all-gather.15
  319.4 13.1 reduce-scatter.6
  345.2 13.3 all-gather.17
  385.9 15.6 reduce-scatter.8
  410.6 13.2 all-gather.19
  589.2 11.9 reduce-scatter.10

commit v2 on v1

--- a/solution.py
+++ b/solution.py
@@ -147,6 +147,11 @@
             jax.ShapeDtypeStruct((seqs, pairs, 2, LEN), jnp.float32),
         ],
         compiler_params=pltpu.CompilerParams(vmem_limit_bytes=56 * 1024 * 1024),
+        cost_estimate=pl.CostEstimate(
+            flops=seqs * pairs * 16 * LEN * LEN * PAIR,
+            transcendentals=seqs * pairs * 2 * LEN * LEN,
+            bytes_accessed=8 * queries.size,
+        ),
         name="attend_forward",
     )(lengths, queries, keys_all, values_turned)
 
@@ -163,49 +168,62 @@
         out_shape=[shape, shape, shape],
         scratch_shapes=[pltpu.VMEM((LEN, PAIR), jnp.float32)] * 2,
         compiler_params=pltpu.CompilerParams(vmem_limit_bytes=56 * 1024 * 1024),
+        cost_estimate=pl.CostEstimate(
+            flops=seqs * pairs * 28 * LEN * LEN * PAIR,
+            transcendentals=seqs * pairs * 2 * LEN * LEN,
+            bytes_accessed=18 * queries.size,
+        ),
         name="attend_backward",
     )(lengths, queries, keys_all, keys_turned, values_all, context, context_grad, stats)
 
 
-def owned_parts(*grads):
+def send_blocks(blocks, axes):
+    return lax.all_to_all(blocks, axes, split_axis=0, concat_axis=0, tiled=True)
+
+
+def gather_rows(rows):
     count = lax.axis_size("dp")
-    pieces, shapes = [], []
-    for grad, dim in grads:
-        cut = grad.shape[:dim] + (count, grad.shape[dim] // count) + grad.shape[dim + 1 :]
-        piece = jnp.moveaxis(grad.astype(jnp.bfloat16).reshape(cut), dim, 0)
-        shapes.append(piece.shape[1:])
-        pieces.append(piece.reshape(count, -1, 128))
-    sent = lax.all_to_all(
-        jnp.concatenate(pieces, axis=1), "dp", split_axis=0, concat_axis=0, tiled=True
-    )
-    summed = jnp.sum(sent.astype(jnp.float32), axis=0)
-    owned, start = [], 0
-    for piece, shape in zip(pieces, shapes):
-        owned.append(summed[start : start + piece.shape[1]].reshape(shape))
-        start += piece.shape[1]
-    return owned
+    blocks = jnp.broadcast_to(rows[None], (count,) + rows.shape)
+    return send_blocks(blocks, "dp").reshape(count * rows.shape[0], rows.shape[1])
+
+
+def send_rows(rows):
+    count = lax.axis_size("dp")
+    return send_blocks(rows.reshape(count, rows.shape[0] // count, rows.shape[1]), "dp")
+
+
+def summed(sent):
+    return jnp.sum(sent.astype(jnp.float32), axis=0)
+
+
+def dot_tn(left, right):
+    return lax.dot_general(
+        left, right, (((0,), (0,)), ((), ())), preferred_element_type=jnp.float32
+    )
 
 
 def body(inputs, out_grad, lengths, w_qkv, w_out, w_up, w_down, gains, shifts, ff_bias):
     score_scale = HD ** (-0.5)
-    seq_count = lengths.shape[0]
-    head_count = w_qkv.shape[2] // HD
     gains_f = gains.astype(jnp.float32)
     shifts_f = shifts.astype(jnp.float32)
     inputs_f = inputs.astype(jnp.float32)
     gathered = lax.all_gather(inputs, "tensor", axis=0, tiled=True)
-    qkv_full, out_full = (
-        lax.all_gather(w_qkv, "dp", axis=1, tiled=True),
-        lax.all_gather(w_out, "dp", axis=1, tiled=True),
-    )
-    projected = jnp.einsum("rd,cde->cre", gathered, qkv_full, preferred_element_type=jnp.float32)
-    queries = (projected[0] * score_scale).astype(jnp.bfloat16)
-    keys_all = projected[1].astype(jnp.bfloat16)
-    values_all = projected[2].astype(jnp.bfloat16)
+    width = w_qkv.shape[2]
+    own_first = jnp.concatenate([w_qkv[0], w_qkv[1], w_qkv[2], w_out.T], axis=1)
+    first = gather_rows(own_first)
+    own_up, first = lax.optimization_barrier((w_up, first))
+    up_full = gather_rows(own_up)
+    qkv_full, out_turned = first[:, : 3 * width], first[:, 3 * width :]
+    projected = dot_nn(gathered, qkv_full)
+    queries = (projected[:, :width] * score_scale).astype(jnp.bfloat16)
+    keys_all = projected[:, width : 2 * width].astype(jnp.bfloat16)
+    values_all = projected[:, 2 * width :].astype(jnp.bfloat16)
     context, stats = attend(lengths, queries, keys_all, values_all.T)
+    own_down, up_full, context = lax.optimization_barrier((w_down.T, up_full, context))
+    down_turned = gather_rows(own_down)
     attn_branch = (
         lax.psum_scatter(
-            jnp.dot(context, out_full, preferred_element_type=jnp.float32),
+            dot_nt(context, out_turned),
             "tensor",
             scatter_dimension=0,
             tiled=True,
@@ -216,10 +234,6 @@
     normed_f, norm_one_back = jax.vjp(layer_norm, resid_one, gains_f[0], shifts_f[1])
     normed_one = normed_f.astype(jnp.bfloat16)
     normed_all = lax.all_gather(normed_one, "tensor", axis=0, tiled=True)
-    up_full, down_full = (
-        lax.all_gather(w_up, "dp", axis=0, tiled=True),
-        lax.all_gather(w_down, "dp", axis=1, tiled=True),
-    )
     ff_pre = jnp.dot(normed_all, up_full, preferred_element_type=jnp.float32) + ff_bias.astype(
         jnp.float32
     )
@@ -227,7 +241,7 @@
     ff_act = ff_act_f.astype(jnp.bfloat16)
     mlp_branch = (
         lax.psum_scatter(
-            jnp.dot(ff_act, down_full, preferred_element_type=jnp.float32),
+            dot_nt(ff_act, down_turned),
             "tensor",
             scatter_dimension=0,
             tiled=True,
@@ -240,8 +254,10 @@
     mlp_grad = resid_two_grad.astype(jnp.bfloat16)
     shift_two_grad = jnp.sum(mlp_grad.astype(jnp.float32), axis=0)
     mlp_grad_all = lax.all_gather(mlp_grad, "tensor", axis=0, tiled=True)
-    act_grad = jnp.einsum("rd,fd->rf", mlp_grad_all, down_full, preferred_element_type=jnp.float32)
-    down_grad = jnp.einsum("rf,rd->fd", ff_act, mlp_grad_all, preferred_element_type=jnp.float32)
+    down_grad = dot_tn(mlp_grad_all, ff_act).astype(jnp.bfloat16)
+    down_grad, mlp_grad_all = lax.optimization_barrier((down_grad, mlp_grad_all))
+    down_sent = send_rows(down_grad)
+    act_grad = dot_nn(mlp_grad_all, down_turned)
     pre_grad = gelu_back(act_grad)[0].astype(jnp.bfloat16)
     bias_grad = jnp.sum(pre_grad.astype(jnp.float32), axis=0)
     up_grad = jnp.einsum("rd,rf->df", normed_all, pre_grad, preferred_element_type=jnp.float32)
@@ -256,41 +272,54 @@
     attn_grad = resid_one_grad.astype(jnp.bfloat16)
     shift_zero_grad = jnp.sum(attn_grad.astype(jnp.float32), axis=0)
     attn_grad_all = lax.all_gather(attn_grad, "tensor", axis=0, tiled=True)
-    context_grad = jnp.einsum(
-        "rd,ed->re", attn_grad_all, out_full, preferred_element_type=jnp.float32
-    ).astype(jnp.bfloat16)
-    out_proj_grad = jnp.einsum(
-        "re,rd->ed", context, attn_grad_all, preferred_element_type=jnp.float32
-    )
-    down_owned, up_owned, out_owned = owned_parts(
-        (down_grad, 1), (up_grad, 0), (out_proj_grad, 1)
-    )
-    stacked_grad = jnp.stack(
-        attend_back(
-            lengths, queries, keys_all, keys_all.T, values_all, context, context_grad, stats
-        )
-    )
-    qkv_grad = jnp.einsum("rd,cre->cde", gathered, stacked_grad, preferred_element_type=jnp.float32)
-    (qkv_owned,) = owned_parts((qkv_grad, 1))
+    context_grad = dot_nn(attn_grad_all, out_turned).astype(jnp.bfloat16)
+    out_proj_grad = dot_tn(attn_grad_all, context)
+    tensor_count = lax.axis_size("tensor")
+    dp_count = lax.axis_size("dp")
+    small = jnp.concatenate(
+        [
+            gain_one_grad, gain_two_grad, shift_zero_grad, shift_one_grad, shift_two_grad,
+            shift_three_grad, bias_grad,
+        ]
+    )
+    packed = jnp.concatenate(
+        [up_grad.astype(jnp.bfloat16), out_proj_grad.astype(jnp.bfloat16)], axis=1
+    )
+    packed, small, down_sent, context_grad = lax.optimization_barrier(
+        (packed, small, down_sent, context_grad)
+    )
+    packed_sent = send_rows(packed)
+    hidden = w_up.shape[1]
+    devices = dp_count * tensor_count
+    small_all = send_blocks(
+        jnp.broadcast_to(small[None], (devices,) + small.shape), ("dp", "tensor")
+    )
+    features = 6 * inputs.shape[1]
+    feature_sum = jnp.sum(small_all[:, :features], axis=0).reshape(6, inputs.shape[1])
+    gain_sum, shift_sum = feature_sum[:2], feature_sum[2:]
+    own_slot = (jnp.arange(tensor_count, dtype=jnp.int32) == lax.axis_index("tensor")).astype(
+        jnp.float32
+    )
+    bias_all = small_all[:, features:].reshape(dp_count, tensor_count, hidden)
+    bias_owned = jnp.sum(bias_all * own_slot[None, :, None], axis=(0, 1))
+    stacked_grad = attend_back(
+        lengths, queries, keys_all, keys_all.T, values_all, context, context_grad, stats
+    )
+    packed_sent, stacked_grad = lax.optimization_barrier((packed_sent, stacked_grad))
+    stacked_grad = jnp.concatenate(stacked_grad, axis=1)
+    down_owned = summed(down_sent).T
+    packed_owned = summed(packed_sent)
+    up_owned, out_owned = packed_owned[:, :hidden], packed_owned[:, hidden:].T
+    qkv_rows = summed(send_rows(dot_tn(gathered, stacked_grad).astype(jnp.bfloat16)))
+    qkv_owned = qkv_rows.reshape(-1, 3, width).transpose(1, 0, 2)
     slab_rows = stacked_grad
-    parts = jnp.einsum("cre,cde->rd", slab_rows, qkv_full, preferred_element_type=jnp.float32)
+    parts = dot_nt(slab_rows, qkv_full)
     input_grad = resid_one_grad + lax.psum_scatter(
         parts.astype(jnp.bfloat16),
         "tensor",
         scatter_dimension=0,
         tiled=True,
     ).astype(jnp.float32)
-    gain_grads = jnp.stack([gain_one_grad, gain_two_grad])
-    shift_grads = jnp.stack([shift_zero_grad, shift_one_grad, shift_two_grad, shift_three_grad])
-    tensor_count = lax.axis_size("tensor")
-    own_slot = (jnp.arange(tensor_count, dtype=jnp.int32) == lax.axis_index("tensor")).astype(
-        jnp.float32
-    )
-    spread_bias = own_slot[:, None] * bias_grad[None, :]
-    gain_sum, shift_sum, bias_sum = lax.psum(
-        (gain_grads, shift_grads, spread_bias), ("dp", "tensor")
-    )
-    bias_owned = jnp.sum(own_slot[:, None] * bias_sum, axis=0)
     return (
         result.astype(jnp.bfloat16),
         input_grad,

time: 751 us -> 567 us (0.75)
  blocking collectives: 165 us -> 0 us
  waiting for transfers between devices: 216 us -> 183 us
  starting transfers between devices: 16.2 us -> 44.8 us
  local copies, waits for them, and re-layouts: 48 us -> 33.5 us
    all_gather x3 -> x0, waiting for transfers between devices: 134 us -> none  [the longest x1 60.4 us: body(): lax.all_gather(w_up, 'dp', axis=0, tiled=True)]
    psum x1 -> x0, blocking collectives: 131 us -> none  [body(): lax.psum((gain_grads, shift_grads, spread_bias), ('dp', 'tensor'))]
    all_to_all x2 -> x7, waiting for transfers between devices: 0.01 us -> 122 us  [send_blocks(): return lax.all_to_all(blocks, axes, split_axis=0, concat_axis=0, tiled=True)]
    all_gather x1 -> x0, blocking collectives: 34.5 us -> none  [body(): lax.all_gather(w_out, 'dp', axis=1, tiled=True)]
    all_to_all x2 -> x7, starting transfers between devices: 14.8 us -> 43.6 us  [send_blocks(): return lax.all_to_all(blocks, axes, split_axis=0, concat_axis=0, tiled=True)]
    reshape x12 -> x1, local copies, waits for them, and re-layouts: 24.8 us -> 1.02 us  [body(): qkv_owned = qkv_rows.reshape(-1, 3, width).transpose(1, 0, 2)]
    all_gather x1, waiting for transfers between devices: 12.9 us -> 4.79 us  [body(): normed_all = lax.all_gather(normed_one, 'tensor', axis=0, tiled=True)]
    all_gather x1, waiting for transfers between devices: 11.8 us -> 4.05 us  [body(): attn_grad_all = lax.all_gather(attn_grad, 'tensor', axis=0, tiled=True)]
  transfers between devices with their start and end apart: 13 -> 15, of which waited for: 9 -> 11; matrix products, arithmetic and copies ran while one was open for 15% -> 19% of each run, Pallas kernels for 0% -> 21%
where the time goes in v2:
time: 567 us; the launch traced here: 558 us
  waiting for transfers between devices  183 us (32%)
  matrix products  125 us (22%)
  Pallas kernels  119 us (21%)
  starting transfers between devices  44.8 us (8%)
  other arithmetic  38.2 us (7%)
  local copies, waits for them, and re-layouts  33.5 us (6%)
  between operations  15.4 us (3%)
    all_to_all x7, waiting for transfers between devices, send_blocks(): return lax.all_to_all(blocks, axes, split_axis=0, concat_axis=0, tiled=True)  122 us
    pallas_call x1, Pallas kernels, attend_back(): pl.pallas_call(backward_kernel, grid=(seqs, pairs, LEN // QUERY_ROWS), in...  73.4 us
    pallas_call x1, Pallas kernels, attend(): pl.pallas_call(forward_kernel, grid=(seqs, pairs, LEN // QUERY_ROWS), in_...  45.8 us
    all_to_all x7, starting transfers between devices, send_blocks(): return lax.all_to_all(blocks, axes, split_axis=0, concat_axis=0, tiled=True)  43.6 us
    dot_general x1, matrix products, body(): jnp.dot(normed_all, up_full, preferred_element_type=jnp.float32)  34.8 us
    dot_general x3, matrix products, dot_nn(): return jnp.dot(left, right, preferred_element_type=jnp.float32)  27.6 us
    dot_general x3, matrix products, dot_tn(): lax.dot_general(left, right, (((0,), (0,)), ((), ())), preferred_element_...  23 us
    dot_general x3, matrix products, dot_nt(): lax.dot_general(left, right, (((1,), (1,)), ((), ())), preferred_element_...  21.3 us
  transfers between devices with their start and end apart: 15, of which 11 were waited for; matrix products, arithmetic and copies ran while one was open for 19% of the time, Pallas kernels for 21%

profile of v2, /device:TPU:12, one launch (start us, length us, event | category | flops | bytes accessed | tf_op | source)
XLA Modules:
  0.0 558.3 jit_solution(12576461715365350347)
XLA Ops:
  10.4 7.3 %all-to-all-start = ((bf16[16,48,1536]{2,1,0:T(8,128)(2,1)}), bf16[16,48,1536]{2,1,0:T(8,128)(2,1)S(1)}, u32[]{:S(2)}, u32[]{:S(2)}) async-start(bf16[16,48,1536]{2,1,0:T(8,128)(2,1)} %broadcast_in_dim.16), calls=%async_computation | async-start | bytes 4718592 | tf_op jit(solution)/shard_map/all_to_all | solution.py:181
  19.1 52.3 %all-to-all-done = bf16[16,48,1536]{2,1,0:T(8,128)(2,1)S(1)} async-done(((bf16[16,48,1536]{2,1,0:T(8,128)(2,1)}), bf16[16,48,1536]{2,1,0:T(8,128)(2,1)S(1)}, u32[]{:S(2)}, u32[]{:S(2)}) %all-to-all-start) | async-done | bytes 2359328 | tf_op jit(solution)/shard_map/all_to_all | solution.py:181
  71.5 1.9 broadcast_in_dim.17
  73.3 4.9 all-to-all-start.1
  78.3 9.8 %fusion.25 = (bf16[2048,1152]{1,0:T(8,128)(2,1)S(1)}, f32[2048,1152]{1,0:T(8,128)}) fusion(bf16[2048,768]{1,0:T(8,128)(2,1)} %all-gather.5.cloned.1.call-done, bf16[768,1536]{1,0:T(8,128)(2,1)S(1)} %bitcast.50), kind=kOutput, calls=%fused_computation.102 | convolution fusion | flops 3626237952 | bytes 19070976 | tf_op jit(solution)/shard_map/dot_general | solution.py:44
  88.1 2.4 fusion.24
  92.1 3.3 fusion.10.q_ref
  95.4 45.8 %attend_forward.1 = (bf16[2048,384]{1,0:T(8,128)(2,1)}, f32[1,3,2,2048]{3,2,1,0:T(2,128)}) custom-call(s32[1]{0:T(128)S(6)} %copy.52.lens_ref, bf16[2048,384]{1,0:T(8,128)(2,1)} %fusion.10.q_ref, bf16[2048,384]{1,0:T(8,128)(2,1)} %get-tuple-element.106.k_ref, bf16[384,2048]{1,0:T(8,128)(2,1)} %copy.34.vt_ref), custom_call_target="tpu_custom_call" | custom-call | flops 25769803776 | bytes 6291456 | tf_op jit(solution)/shard_map/attend_forward/pallas_call | solution.py:140
  141.2 6.0 %fusion.14 = f32[2048,768]{1,0:T(8,128)} fusion(bf16[2048,384]{1,0:T(8,128)(2,1)} %get-tuple-element.32.ctx_ref, bf16[768,1536]{1,0:T(8,128)(2,1)} %bitcast.51), kind=kOutput, calls=%fused_computation.59 | convolution fusion | flops 1207959552 | bytes 8454144 | tf_op jit(solution)/shard_map/dot_general | solution.py:38
  148.0 15.0 %reduce-scatter.5.cloned.1.call-done = f32[1024,768]{1,0:T(8,128)} async-done(((f32[2048,768]{1,0:T(8,128)}), f32[1024,768]{1,0:T(8,128)}) %reduce-scatter.5.cloned.1.call-update) | async-done | bytes 3145744 | tf_op jit(solution)/shard_map/reduce_scatter | solution.py:225
  163.0 2.8 fusion.23
  170.3 7.0 %all-to-all-start.2 = ((bf16[16,48,1536]{2,1,0:T(8,128)(2,1)}), bf16[16,48,1536]{2,1,0:T(8,128)(2,1)}, u32[]{:S(2)}, u32[]{:S(2)}) async-start(bf16[16,48,1536]{2,1,0:T(8,128)(2,1)} %broadcast_in_dim.18), calls=%async_computation.3 | async-start | bytes 4718592 | tf_op jit(solution)/shard_map/all_to_all | solution.py:181
  177.3 4.8 all-gather.7.cloned.1.call-done
  182.1 34.8 %multiply_convert_fusion = (bf16[2048,1536]{1,0:T(8,128)(2,1)}, f32[2048,1536]{1,0:T(8,128)}, f32[2048,1536]{1,0:T(8,128)}) fusion(f32[1536]{0:T(1024)S(1)} %convert_element_type.96, bf16[2048,768]{1,0:T(8,128)(2,1)} %all-gather.7.cloned.1.call-done, bf16[768,1536]{1,0:T(8,128)(2,1)} %bitcast.6), kind=kOutput, calls=%fused_computation.4 | convolution fusion | flops 5039456256 | bytes 36968448 | tf_op jit(solution)/shard_map/dot_general | solution.py:237
  216.9 14.3 %all-to-all-done.2 = bf16[16,48,1536]{2,1,0:T(8,128)(2,1)} async-done(((bf16[16,48,1536]{2,1,0:T(8,128)(2,1)}), bf16[16,48,1536]{2,1,0:T(8,128)(2,1)}, u32[]{:S(2)}, u32[]{:S(2)}) %all-to-all-start.2) | async-done | bytes 2359328 | tf_op jit(solution)/shard_map/all_to_all | solution.py:181
  231.3 9.6 %fusion.26 = f32[2048,768]{1,0:T(8,128)} fusion(bf16[2048,1536]{1,0:T(8,128)(2,1)} %get-tuple-element.99, bf16[768,1536]{1,0:T(8,128)(2,1)} %bitcast.9), kind=kOutput, calls=%fused_computation.103 | convolution fusion | flops 4831838208 | bytes 14942208 | tf_op jit(solution)/shard_map/dot_general | solution.py:38
  241.2 14.2 %reduce-scatter.7.cloned.1.call-done = f32[1024,768]{1,0:T(8,128)} async-done(((f32[2048,768]{1,0:T(8,128)}), f32[1024,768]{1,0:T(8,128)}) %reduce-scatter.7.cloned.1.call-update) | async-done | bytes 3145744 | tf_op jit(solution)/shard_map/reduce_scatter | solution.py:243
  255.4 2.9 fusion.21
  261.0 2.6 fusion.20
  266.8 13.4 %all-gather.9.cloned.1.call-done = bf16[2048,768]{1,0:T(8,128)(2,1)} async-done(((bf16[1024,768]{1,0:T(8,128)(2,1)}), bf16[2048,768]{1,0:T(8,128)(2,1)}) %all-gather.9.cloned.1.call-update) | async-done | bytes 3145744 | tf_op jit(solution)/shard_map/all_gather | solution.py:256
  280.2 9.9 %convolution_convert_fusion.2 = bf16[768,1536]{1,0:T(8,128)(2,1)} fusion(bf16[2048,768]{1,0:T(8,128)(2,1)} %all-gather.9.cloned.1.call-done, bf16[2048,1536]{1,0:T(8,128)(2,1)} %get-tuple-element.99), kind=kOutput, calls=%fused_computation.31 | convolution fusion | flops 4833017856 | bytes 11796480 | tf_op jit(solution)/shard_map/dot_general | solution.py:200
  290.1 13.8 %convert_reduce_fusion = (f32[1536]{0:T(1024)S(1)}, bf16[2048,1536]{1,0:T(8,128)(2,1)S(1)}) fusion(f32[2048,1536]{1,0:T(8,128)} %get-tuple-element.100, bf16[2048,768]{1,0:T(8,128)(2,1)S(1)} %copy-done.20, bf16[768,1536]{1,0:T(8,128)(2,1)} %bitcast.9, f32[2048,1536]{1,0:T(8,128)} %get-tuple-element.113, f32[1536]{0:T(1024)S(1)} %convert_element_type.96), kind=kOutput, calls=%fused_computation.2 | convolution fusion | flops 4885314048 | bytes 36974592 | tf_op jit(solution)/shard_map/dot_general | solution.py:44
  303.9 2.7 copy-done.21
  306.6 8.6 %fusion.27 = f32[2048,768]{1,0:T(8,128)} fusion(bf16[2048,1536]{1,0:T(8,128)(2,1)S(1)} %get-tuple-element.115, bf16[768,1536]{1,0:T(8,128)(2,1)} %bitcast.6), kind=kOutput, calls=%fused_computation.104 | convolution fusion | flops 4831838208 | bytes 14942208 | tf_op jit(solution)/shard_map/rf,df->rd/dot_general | solution.py:266
  315.2 7.0 %all-to-all-start.3 = ((bf16[16,48,1536]{2,1,0:T(8,128)(2,1)}), bf16[16,48,1536]{2,1,0:T(8,128)(2,1)}, u32[]{:S(2)}, u32[]{:S(2)}) async-start(bf16[16,48,1536]{2,1,0:T(8,128)(2,1)} %bitcast.56), calls=%async_computation.6 | async-start | bytes 4718592 | tf_op jit(solution)/shard_map/all_to_all | solution.py:181
  322.6 8.4 %reduce-scatter.9.cloned.1.call-done = f32[1024,768]{1,0:T(8,128)} async-done(((f32[2048,768]{1,0:T(8,128)}), f32[1024,768]{1,0:T(8,128)}) %reduce-scatter.9.cloned.1.call-update) | async-done | bytes 3145744 | tf_op jit(solution)/shard_map/reduce_scatter | solution.py:265
  331.0 3.7 multiply_reduce_fusion
  339.4 9.3 %convolution_convert_fusion.1 = bf16[768,1536]{1,0:T(8,128)(2,1)} fusion(bf16[2048,768]{1,0:T(8,128)(2,1)} %all-gather.7.cloned.1.call-done, bf16[2048,1536]{1,0:T(8,128)(2,1)} %copy-done.21), kind=kOutput, calls=%fused_computation.30 | convolution fusion | flops 4833017856 | bytes 11796480 | tf_op jit(solution)/shard_map/rd,rf->df/dot_general | solution.py:263
  348.8 4.0 all-gather.11.cloned.1.call-done
  352.9 3.8 convolution_convert_fusion.5
  356.8 1.8 pad_maximum_fusion
  359.7 4.1 convolution_convert_fusion.4.grad_ref
  363.8 12.3 %all-to-all-done.3 = bf16[16,48,1536]{2,1,0:T(8,128)(2,1)} async-done(((bf16[16,48,1536]{2,1,0:T(8,128)(2,1)}), bf16[16,48,1536]{2,1,0:T(8,128)(2,1)}, u32[]{:S(2)}, u32[]{:S(2)}) %all-to-all-start.3) | async-done | bytes 2359328 | tf_op jit(solution)/shard_map/all_to_all | solution.py:181
  376.1 5.6 %all-to-all-start.4 = ((bf16[16,48,1920]{2,1,0:T(8,128)(2,1)}), bf16[16,48,1920]{2,1,0:T(8,128)(2,1)S(1)}, u32[]{:S(2)}, u32[]{:S(2)}) async-start(bf16[16,48,1920]{2,1,0:T(8,128)(2,1)} %bitcast.49), calls=%async_computation.7 | async-start | bytes 5898240 | tf_op jit(solution)/shard_map/all_to_all | solution.py:181
  382.0 2.6 copy.36.kt_ref
  384.6 73.4 %attend_backward.1 = (bf16[2048,384]{1,0:T(8,128)(2,1)}, bf16[2048,384]{1,0:T(8,128)(2,1)}, bf16[2048,384]{1,0:T(8,128)(2,1)}) custom-call(s32[1]{0:T(128)S(6)} %copy.52.lens_ref, bf16[2048,384]{1,0:T(8,128)(2,1)} %fusion.10.q_ref, bf16[2048,384]{1,0:T(8,128)(2,1)} %get-tuple-element.106.k_ref, bf16[384,2048]{1,0:T(8,128)(2,1)} %copy.36.kt_ref, ...), custom_call_target="tpu_custom_call" | custom-call | flops 45097156608 | bytes 14155776 | tf_op jit(solution)/shard_map/attend_backward/pallas_call | solution.py:163
  458.1 2.7 constant_dynamic-update-slice_fusion.3
  461.8 2.1 copy-done.12
  463.9 5.6 %convolution_convert_fusion = bf16[2048,768]{1,0:T(8,128)(2,1)} fusion(bf16[2048,1152]{1,0:T(8,128)(2,1)S(1)} %constant_dynamic-update-slice_fusion.1, bf16[768,1536]{1,0:T(8,128)(2,1)S(1)} %bitcast.53), kind=kOutput, calls=%fused_computation.29 | convolution fusion | flops 3625451520 | bytes 9633792 | tf_op jit(solution)/shard_map/dot_general | solution.py:38
  470.8 6.1 %all-to-all-start.6 = ((f32[32,1,6144]{2,1,0:T(1,128)}), f32[32,1,6144]{2,1,0:T(1,128)S(1)}, u32[]{:S(2)}, u32[]{:S(2)}) async-start(f32[32,1,6144]{2,1,0:T(1,128)} %broadcast_in_dim.23), calls=%async_computation.10 | async-start | bytes 1572864 | tf_op jit(solution)/shard_map/all_to_all | solution.py:181
  476.9 9.2 %convolution_convert_fusion.3 = bf16[1152,768]{0,1:T(8,128)(2,1)} fusion(bf16[2048,1152]{1,0:T(8,128)(2,1)} %copy-done.12, bf16[2048,768]{1,0:T(8,128)(2,1)} %all-gather.5.cloned.1.call-done), kind=kOutput, calls=%fused_computation.32 | convolution fusion | flops 3624763392 | bytes 9633792 | tf_op jit(solution)/shard_map/dot_general | solution.py:200
  486.1 10.4 %all-to-all-done.6 = f32[32,1,6144]{2,1,0:T(1,128)S(1)} async-done(((f32[32,1,6144]{2,1,0:T(1,128)}), f32[32,1,6144]{2,1,0:T(1,128)S(1)}, u32[]{:S(2)}, u32[]{:S(2)}) %all-to-all-start.6) | async-done | bytes 786464 | tf_op jit(solution)/shard_map/all_to_all | solution.py:181
  496.5 5.7 %all-to-all-start.5 = ((bf16[16,48,1152]{2,1,0:T(8,128)(2,1)}), bf16[16,48,1152]{2,1,0:T(8,128)(2,1)}, u32[]{:S(2)}, u32[]{:S(2)}) async-start(bf16[16,48,1152]{2,1,0:T(8,128)(2,1)} %bitcast.14), calls=%async_computation.9 | async-start | bytes 3538944 | tf_op jit(solution)/shard_map/all_to_all | solution.py:181
  502.3 2.7 convert_reduce_fusion.3
  507.3 2.5 convert_reduce_fusion.1
  511.1 32.6 %all-to-all-done.5 = bf16[16,48,1152]{2,1,0:T(8,128)(2,1)} async-done(((bf16[16,48,1152]{2,1,0:T(8,128)(2,1)}), bf16[16,48,1152]{2,1,0:T(8,128)(2,1)}, u32[]{:S(2)}, u32[]{:S(2)}) %all-to-all-start.5) | async-done | bytes 1769504 | tf_op jit(solution)/shard_map/all_to_all | solution.py:181
  543.7 2.4 convert_reduce_fusion.4
  547.8 3.4 convert_add_fusion
  (112 shorter events, 31.3 us)
Async XLA Ops:
  10.4 61.0 %copy-start.13 = (bf16[48,1536]{1,0:T(8,128)(2,1)S(1)}, bf16[48,1536]{1,0:T(8,128)(2,1)}, u32[]{:S(2)}) copy-start(bf16[48,1536]{1,0:T(8,128)(2,1)} %param.15) | copy-start | bytes 442372
  10.4 61.0 %all-to-all-start = ((bf16[16,48,1536]{2,1,0:T(8,128)(2,1)}), bf16[16,48,1536]{2,1,0:T(8,128)(2,1)S(1)}, u32[]{:S(2)}, u32[]{:S(2)}) async-start(bf16[16,48,1536]{2,1,0:T(8,128)(2,1)} %broadcast_in_dim.16), calls=%async_computation | async-start | bytes 4718592 | tf_op jit(solution)/shard_map/all_to_all | solution.py:181
  17.7 60.6 %all-gather.5.cloned.1.call-start = ((), (), s32[]{:S(2)}) async-start(), calls=%async_computation.11 | async-start | bytes 4718592 | tf_op jit(solution)/shard_map/all_gather | solution.py:210
  71.4 6.8 %copy-start.6 = (bf16[16,48,1536]{2,1,0:T(8,128)(2,1)}, bf16[16,48,1536]{2,1,0:T(8,128)(2,1)S(1)}, u32[]{:S(2)}) copy-start(bf16[16,48,1536]{2,1,0:T(8,128)(2,1)S(1)} %all-to-all-done) | copy-start | bytes 7077892
  73.3 67.8 %all-to-all-start.1 = ((bf16[16,48,1536]{2,1,0:T(8,128)(2,1)}), bf16[16,48,1536]{2,1,0:T(8,128)(2,1)}, u32[]{:S(2)}, u32[]{:S(2)}) async-start(bf16[16,48,1536]{2,1,0:T(8,128)(2,1)} %broadcast_in_dim.17), calls=%async_computation.1 | async-start | bytes 4718592 | tf_op jit(solution)/shard_map/all_to_all | solution.py:181
  78.2 84.7 %reduce-scatter.5.cloned.1.call-start = ((), (), s32[]{:S(2)}) async-start(), calls=%async_computation.12 | async-start | bytes 9437184 | tf_op jit(solution)/shard_map/reduce_scatter | solution.py:225
  147.2 0.7 copy-start.17
  147.2 0.7 copy-start.19
  147.2 34.9 %all-gather.7.cloned.1.call-start = ((), (), s32[]{:S(2)}) async-start(), calls=%async_computation.13 | async-start | bytes 4718592 | tf_op jit(solution)/shard_map/all_gather | solution.py:236
  166.3 0.6 copy-start.15
  166.9 1.7 copy-start.18
  166.9 1.7 copy-start.14
  170.3 61.0 %all-to-all-start.2 = ((bf16[16,48,1536]{2,1,0:T(8,128)(2,1)}), bf16[16,48,1536]{2,1,0:T(8,128)(2,1)}, u32[]{:S(2)}, u32[]{:S(2)}) async-start(bf16[16,48,1536]{2,1,0:T(8,128)(2,1)} %broadcast_in_dim.18), calls=%async_computation.3 | async-start | bytes 4718592 | tf_op jit(solution)/shard_map/all_to_all | solution.py:181
  177.2 78.1 %reduce-scatter.7.cloned.1.call-start = ((), (), s32[]{:S(2)}) async-start(), calls=%async_computation.14 | async-start | bytes 9437184 | tf_op jit(solution)/shard_map/reduce_scatter | solution.py:243
  240.9 39.3 %all-gather.9.cloned.1.call-start = ((), (), s32[]{:S(2)}) async-start(), calls=%async_computation.15 | async-start | bytes 4718592 | tf_op jit(solution)/shard_map/all_gather | solution.py:256
  258.3 1.4 copy-start.5
  263.6 1.7 copy-start.2
  266.8 64.2 %reduce-scatter.9.cloned.1.call-start = ((), (), s32[]{:S(2)}) async-start(), calls=%async_computation.16 | async-start | bytes 9437184 | tf_op jit(solution)/shard_map/reduce_scatter | solution.py:265
  280.2 9.9 %copy-start.20 = (bf16[2048,768]{1,0:T(8,128)(2,1)S(1)}, bf16[2048,768]{1,0:T(8,128)(2,1)}, u32[]{:S(2)}) copy-start(bf16[2048,768]{1,0:T(8,128)(2,1)} %all-gather.9.cloned.1.call-done) | copy-start | bytes 9437188
  303.9 2.7 copy-start.21
  315.2 61.0 %all-to-all-start.3 = ((bf16[16,48,1536]{2,1,0:T(8,128)(2,1)}), bf16[16,48,1536]{2,1,0:T(8,128)(2,1)}, u32[]{:S(2)}, u32[]{:S(2)}) async-start(bf16[16,48,1536]{2,1,0:T(8,128)(2,1)} %bitcast.56), calls=%async_computation.6 | async-start | bytes 4718592 | tf_op jit(solution)/shard_map/all_to_all | solution.py:181
  322.1 12.5 %copy-start.16 = (f32[1024]{0:T(1024)S(1)}, f32[1024]{0:T(1024)}, u32[]{:S(2)}) copy-start(f32[1024]{0:T(1024)} %copy-done.15) | copy-start | bytes 12292
  322.1 30.7 %all-gather.11.cloned.1.call-start = ((), (), s32[]{:S(2)}) async-start(), calls=%async_computation.17 | async-start | bytes 4718592 | tf_op jit(solution)/shard_map/all_gather | solution.py:274
  336.2 1.7 copy-start
  339.4 13.5 %copy-start.4 = (bf16[2048,384]{1,0:T(8,128)(2,1)S(1)}, bf16[2048,384]{1,0:T(8,128)(2,1)}, u32[]{:S(2)}) copy-start(bf16[2048,384]{1,0:T(8,128)(2,1)} %get-tuple-element.32.ctx_ref) | copy-start | bytes 4718596
  352.9 3.9 copy-start.9
  356.8 3.0 copy-start.8
  376.1 81.9 %all-to-all-start.4 = ((bf16[16,48,1920]{2,1,0:T(8,128)(2,1)}), bf16[16,48,1920]{2,1,0:T(8,128)(2,1)S(1)}, u32[]{:S(2)}, u32[]{:S(2)}) async-start(bf16[16,48,1920]{2,1,0:T(8,128)(2,1)} %bitcast.49), calls=%async_computation.7 | async-start | bytes 5898240 | tf_op jit(solution)/shard_map/all_to_all | solution.py:181
  381.8 166.1 %reduce-scatter.11.cloned.1.call-start = ((), (), s32[]{:S(2)}) async-start(), calls=%async_computation.18 | async-start | bytes 4718592 | tf_op jit(solution)/shard_map/reduce_scatter | solution.py:317
  458.0 3.3 copy-start.3
  458.0 2.9 copy-start.11
  458.0 3.4 copy-start.10
  461.0 2.9 copy-start.7
  461.8 2.1 copy-start.12
  470.8 25.7 %all-to-all-start.6 = ((f32[32,1,6144]{2,1,0:T(1,128)}), f32[32,1,6144]{2,1,0:T(1,128)S(1)}, u32[]{:S(2)}, u32[]{:S(2)}) async-start(f32[32,1,6144]{2,1,0:T(1,128)} %broadcast_in_dim.23), calls=%async_computation.10 | async-start | bytes 1572864 | tf_op jit(solution)/shard_map/all_to_all | solution.py:181
  496.5 47.2 %all-to-all-start.5 = ((bf16[16,48,1152]{2,1,0:T(8,128)(2,1)}), bf16[16,48,1152]{2,1,0:T(8,128)(2,1)}, u32[]{:S(2)}, u32[]{:S(2)}) async-start(bf16[16,48,1152]{2,1,0:T(8,128)(2,1)} %bitcast.14), calls=%async_computation.9 | async-start | bytes 3538944 | tf_op jit(solution)/shard_map/all_to_all | solution.py:181
  507.3 40.5 %copy-start.1 = (f32[1024,768]{1,0:T(8,128)S(1)}, f32[1024,768]{1,0:T(8,128)}, u32[]{:S(2)}) copy-start(f32[1024,768]{1,0:T(8,128)} %copy-done) | copy-start | bytes 9437188
Sparse Core Ops, SparseCore 0:
  20.1 13.2 all-gather.4
  147.3 15.5 reduce-scatter.4
  168.7 13.3 all-gather.6
  241.0 14.3 reduce-scatter.6
  266.9 13.2 all-gather.8
  315.3 15.6 reduce-scatter.8
  339.5 13.3 all-gather.10
  469.7 11.9 reduce-scatter.10
